TPU v7x, 256 devices: a whole 4x4x8 slice. The times are simulated.
256 devices in a mesh: lat: 16 (over x, y), lon: 16 (over z, core).
Axes of the slice: x: 4, y: 4, z: 8, core: 2. Of those that a mesh axis runs over, the one named last changes fastest.
Arguments:
- features: bfloat16 [256, 1440, 256], P('lat', 'lon'), may hold values from -6 to 6
- cotangent: bfloat16 [256, 1440, 256], P('lat', 'lon'), may hold values from -6 to 6
- disco_basis: bfloat16 [3, 256, 3, 33], replicated, may hold values from -0.875 to 0.875
- support_width: int32 [256], replicated, may hold values from 1 to 16, as said below
- mix_weight: bfloat16 [3, 256, 256], replicated, may hold values from -0.21875 to 0.21875
- spectral_filter: float32 [2, 720, 256], replicated, may hold values from -6 to 6
Outputs:
- block_output: bfloat16 [256, 1440, 256], P('lat', 'lon')
- grad_input: bfloat16 [256, 1440, 256], P('lat', 'lon')
- grad_weight: float32 [3, 256, 256], replicated
- grad_filter: float32 [2, 720, 256], replicated
Inputs may be any that keep to these rules, and one draw needn't show every extreme that they name: `support_width`: longitude half-width in cells of the DISCO support at each latitude row.
All inputs are finite; a program needn't handle non-finite values.
Results may differ from a plain program's by a relative error of at most 0.0076.
Values may be sent and summed in bfloat16 or wider, within the bound.
A program may use at most 128 MiB of HBM per device.

v0:
```python
import math

import jax
import jax.numpy as jnp
from jax import lax
from jax.sharding import PartitionSpec as P


def extended(value, sides, width, wrap):
    for axis, dim in sides:
        size, length = (lax.axis_size(axis), value.shape[dim])
        up = [(i, (i + 1) % size) for i in range(size if wrap else size - 1)]
        down = [(j, i) for i, j in up]
        last = lax.slice_in_dim(value, length - width, length, axis=dim)
        initial = lax.slice_in_dim(value, 0, width, axis=dim)
        before = lax.ppermute(last, axis, up)
        after = lax.ppermute(initial, axis, down)
        value = jnp.concatenate([before, value, after], axis=dim)
    return value


def masked_basis(disco_basis, support_width):
    spread = disco_basis.shape[3] // 2
    offsets = jnp.abs(jnp.arange(2 * spread + 1, dtype=jnp.int32) - spread)
    retained = offsets[None, :] <= support_width[:, None]
    return jnp.where(retained[None, :, None, :], disco_basis, jnp.zeros_like(disco_basis))


def band_tables(spread, columns):
    outer = jnp.arange(columns + 2 * spread, dtype=jnp.int32)
    inner = jnp.arange(columns, dtype=jnp.int32)
    taps = jnp.arange(2 * spread + 1, dtype=jnp.int32)
    forward_hot = (outer[:, None, None] - inner[None, :, None] == taps[None, None, :]).astype(
        jnp.float32
    )
    backward_hot = (
        inner[None, :, None] - outer[:, None, None] + 2 * spread == taps[None, None, :]
    ).astype(jnp.float32)
    return (forward_hot, backward_hot)


def dft_tables(longitudes, wavenumbers):
    cell_index = jnp.arange(longitudes, dtype=jnp.int32)
    wave_index = jnp.arange(wavenumbers, dtype=jnp.int32)
    phase_index = wave_index[:, None] * cell_index[None, :] % longitudes
    angles = phase_index.astype(jnp.float32) * (2.0 * math.pi / longitudes)
    cosine_wave = jnp.cos(angles)
    sine_wave = jnp.sin(angles)
    forward_table = jnp.concatenate([cosine_wave, -sine_wave], axis=0).astype(jnp.bfloat16)
    factor = jnp.where(wave_index == 0, 1.0, 2.0).astype(jnp.float32) / longitudes
    inverse_table = jnp.concatenate(
        [cosine_wave * factor[:, None], -sine_wave * factor[:, None]], axis=0
    ).T.astype(jnp.bfloat16)
    return (forward_table, inverse_table)


def silu_slope(values):
    logistic = jax.nn.sigmoid(values)
    return logistic * (1.0 + values * (1.0 - logistic))


def disco_apply(forward_band, input_slab):
    row_count = input_slab.shape[0] - 2
    running = jnp.zeros(
        (forward_band.shape[0], row_count, forward_band.shape[4], input_slab.shape[2]), jnp.float32
    )
    for offset in range(3):
        running = running + jnp.einsum(
            "kiaj,iac->kijc",
            forward_band[:, :, offset],
            input_slab[offset : offset + row_count],
            preferred_element_type=jnp.float32,
        )
    return running.astype(jnp.bfloat16)


def disco_adjoint(backward_band, kernel_grad):
    row_count = kernel_grad.shape[1] - 2
    running = jnp.zeros((row_count, backward_band.shape[4], kernel_grad.shape[3]), jnp.float32)
    for offset in range(3):
        lower = 2 - offset
        running = running + jnp.einsum(
            "kiqb,kiqc->ibc",
            backward_band[:, lower : lower + row_count, offset],
            kernel_grad[:, lower : lower + row_count],
            preferred_element_type=jnp.float32,
        )
    return running


def to_modes(forward_table, field, gain_table):
    spectrum = jnp.einsum("mn,inc->imc", forward_table, field, preferred_element_type=jnp.float32)
    wavenumbers = gain_table.shape[1]
    real_part = spectrum[:, :wavenumbers]
    imag_part = spectrum[:, wavenumbers:]
    real_gain = gain_table[0]
    imag_gain = gain_table[1]
    filtered = jnp.concatenate(
        [
            real_gain * real_part - imag_gain * imag_part,
            real_gain * imag_part + imag_gain * real_part,
        ],
        axis=1,
    ).astype(jnp.bfloat16)
    return (spectrum, filtered)


def from_modes(inverse_table, filtered):
    return jnp.einsum(
        "nm,imc->inc", inverse_table, filtered, preferred_element_type=jnp.float32
    ).astype(jnp.bfloat16)


def adjoint_modes(forward_table, inverse_table, cot_field, spectrum, gain_table):
    wavenumbers = gain_table.shape[1]
    cot_modes = jnp.einsum(
        "nm,inc->imc", inverse_table, cot_field, preferred_element_type=jnp.float32
    )
    real_cot = cot_modes[:, :wavenumbers]
    imag_cot = cot_modes[:, wavenumbers:]
    real_part = spectrum[:, :wavenumbers]
    imag_part = spectrum[:, wavenumbers:]
    real_gain = gain_table[0]
    imag_gain = gain_table[1]
    gradient = jnp.stack(
        [
            jnp.sum(real_cot * real_part + imag_cot * imag_part, axis=0),
            jnp.sum(imag_cot * real_part - real_cot * imag_part, axis=0),
        ]
    )
    back_modes = jnp.concatenate(
        [real_gain * real_cot + imag_gain * imag_cot, real_gain * imag_cot - imag_gain * real_cot],
        axis=1,
    ).astype(jnp.bfloat16)
    spectral_grad = jnp.einsum(
        "mn,imc->inc", forward_table, back_modes, preferred_element_type=jnp.float32
    ).astype(jnp.bfloat16)
    return (gradient, spectral_grad)


def on_device(features, cotangent, disco_basis, support_width, mix_weight, spectral_filter):
    row_count, columns, channels = features.shape
    spread = disco_basis.shape[3] // 2
    wavenumbers = spectral_filter.shape[1]
    lon_devices = lax.axis_size("lon")
    longitudes = columns * lon_devices
    first_row = lax.axis_index("lat") * row_count
    effective = masked_basis(disco_basis, support_width)
    padded_basis = jnp.pad(effective, ((0, 0), (1, 1), (0, 0), (0, 0)))
    local_basis = lax.dynamic_slice_in_dim(padded_basis, first_row, row_count + 2, 1)
    forward_hot, backward_hot = band_tables(spread, columns)
    forward_band = jnp.einsum(
        "kirs,ajs->kiraj", local_basis[:, 1 : row_count + 1].astype(jnp.float32), forward_hot
    ).astype(jnp.bfloat16)
    backward_band = jnp.einsum(
        "kirs,qbs->kirqb", local_basis.astype(jnp.float32), backward_hot
    ).astype(jnp.bfloat16)
    forward_table, inverse_table = dft_tables(longitudes, wavenumbers)
    lat_padded = extended(features, (("lat", 0),), 1, False)
    input_slab = extended(lat_padded, (("lon", 1),), spread, True)
    kernel_out = disco_apply(forward_band, input_slab)
    disco_out = jnp.einsum(
        "kijc,kcd->ijd", kernel_out, mix_weight, preferred_element_type=jnp.float32
    )
    gathered = lax.all_to_all(features, "lon", split_axis=0, concat_axis=1, tiled=True)
    spectrum, filtered = to_modes(forward_table, gathered, spectral_filter)
    spectral = lax.all_to_all(
        from_modes(inverse_table, filtered), "lon", split_axis=1, concat_axis=0, tiled=True
    )
    preact = disco_out + spectral.astype(jnp.float32)
    block_output = (features.astype(jnp.float32) + jax.nn.silu(preact)).astype(jnp.bfloat16)
    pre_grad = (cotangent.astype(jnp.float32) * silu_slope(preact)).astype(jnp.bfloat16)
    mix_part = jnp.einsum("kijc,ijd->kcd", kernel_out, pre_grad, preferred_element_type=jnp.float32)
    cot_field = lax.all_to_all(pre_grad, "lon", split_axis=0, concat_axis=1, tiled=True)
    filter_part, owner_grad = adjoint_modes(
        forward_table, inverse_table, cot_field, spectrum, spectral_filter
    )
    spectral_grad = lax.all_to_all(owner_grad, "lon", split_axis=1, concat_axis=0, tiled=True)
    grad_weight, grad_filter = lax.psum((mix_part, filter_part), ("lat", "lon"))
    products = jnp.einsum(
        "ijd,kcd->kijc", pre_grad, mix_weight, preferred_element_type=jnp.float32
    ).astype(jnp.bfloat16)
    product_rim = extended(products, (("lat", 1),), 1, False)
    kernel_grad = extended(product_rim, (("lon", 2),), spread, True)
    conv_grad = disco_adjoint(backward_band, kernel_grad)
    grad_input = (
        cotangent.astype(jnp.float32) + conv_grad + spectral_grad.astype(jnp.float32)
    ).astype(jnp.bfloat16)
    return (block_output, grad_input, grad_weight, grad_filter)


def solution(mesh):
    return jax.shard_map(
        on_device,
        mesh=mesh,
        in_specs=(P("lat", "lon", None), P("lat", "lon", None), P(), P(), P(), P()),
        out_specs=(P("lat", "lon", None), P("lat", "lon", None), P(), P()),
        check_vma=False,
    )
```

profile of v0, /device:TPU:2, one launch (start us, length us, event | category | flops | bytes accessed | tf_op | source)
XLA Modules:
  0.0 506.2 jit_solution(3732551422688046994)
XLA Ops:
  9.5 8.6 %all-to-all-start = ((bf16[16,90,256]{2,1,0:T(8,128)(2,1)}), bf16[16,90,256]{2,1,0:T(8,128)(2,1)S(1)}, u32[]{:S(2)}, u32[]{:S(2)}) async-start(bf16[16,90,256]{2,1,0:T(8,128)(2,1)} %copy.41), calls=%async_computation | async-start | bytes 1572864 | tf_op jit(solution)/shard_map/all_to_all | solution.py:165
  18.9 3.5 collective-permute-start
  22.4 4.5 collective-permute-start.1
  26.9 20.0 %fusion.5 = (bf16[720,1440]{1,0:T(8,128)(2,1)}, bf16[720,1440]{1,0:T(8,128)(2,1)}) fusion(), kind=kLoop, calls=%fused_computation.13 | loop fusion | flops 12441600 | bytes 4147200 | tf_op jit(solution)/shard_map/convert.12
  47.2 20.2 %multiply_convert_fusion.1 = (bf16[720,1440]{1,0:T(8,128)(2,1)}, bf16[720,1440]{1,0:T(8,128)(2,1)}) fusion(f32[720]{0:T(1024)S(1)} %select_multiply_fusion), kind=kLoop, calls=%fused_computation.7 | loop fusion | flops 14515200 | bytes 4150080 | tf_op jit(solution)/shard_map/convert.6
  71.9 2.8 collective-permute-start.3
  75.8 3.9 fusion.18
  83.3 9.3 %copy.91 = bf16[1,1440,256]{2,0,1:T(2,128)(2,1)} copy(bf16[1,1440,256]{2,1,0:T(8,128)(2,1)S(1)} %fusion.22) | data formatting | bytes 1474560 | tf_op jit(solution)/shard_map/convert_element_type | solution.py:111
  93.2 9.7 %reduce.4 = bf16[1440,256]{1,0:T(8,128)(2,1)} reduce(bf16[1440,1,256]{2,1,0:T(2,128)(2,1)} %bitcast.123, bf16[]{:T(256)} %broadcast.75), dimensions={1}, to_apply=%bitcast.122.reduce_sub_computation | reduce | bytes 1474562
  102.9 2.9 reshape.159
  105.8 7.2 %all-to-all-start.1 = ((bf16[16,2,11520]{2,1,0:T(2,128)(2,1)}), bf16[16,2,11520]{2,1,0:T(2,128)(2,1)}, u32[]{:S(2)}, u32[]{:S(2)}) async-start(bf16[16,2,11520]{2,1,0:T(2,128)(2,1)} %reshape.159), calls=%async_computation.1 | async-start | bytes 1474560 | tf_op jit(solution)/shard_map/all_to_all | solution.py:167
  119.3 13.5 %all-to-all-done.1 = bf16[16,2,11520]{2,1,0:T(2,128)(2,1)} async-done(((bf16[16,2,11520]{2,1,0:T(2,128)(2,1)}), bf16[16,2,11520]{2,1,0:T(2,128)(2,1)}, u32[]{:S(2)}, u32[]{:S(2)}) %all-to-all-start.1) | async-done | bytes 737312 | tf_op jit(solution)/shard_map/all_to_all | solution.py:167
  132.8 5.1 %reshape.160 = bf16[1440,1,256]{2,1,0:T(2,128)(2,1)} reshape(bf16[16,2,11520]{2,1,0:T(2,128)(2,1)} %all-to-all-done.1) | data formatting | bytes 1474560
  137.9 9.8 %convert_reduce_fusion.1 = f32[1440,256]{1,0:T(8,128)} fusion(bf16[1440,1,256]{2,1,0:T(2,128)(2,1)} %reshape.160), kind=kLoop, calls=%fused_computation.53 | loop fusion | flops 368640 | bytes 2211840 | tf_op jit(solution)/shard_map/convert_element_type | solution.py:170
  147.7 2.5 reshape.141
  150.3 5.3 %fusion.29 = (bf16[16,90,256]{2,1,0:T(8,128)(2,1)}, bf16[16,90,256]{2,1,0:T(8,128)(2,1)}) fusion(bf16[16,90,256]{2,0,1:T(8,128)(2,1)} %param.7, bf16[16,90,256]{2,0,1:T(8,128)(2,1)} %param.6, f32[16,90,256]{2,1,0:T(8,128)} %reshape.141, bf16[3,16,90,256]{3,2,0,1:T(8,128)(2,1)} %fusion.24, bf16[3,256,256]{2,1,0:T(8,128)(2,1)S(1)} %copy-done), kind=kOutput, calls=%fused_computation.43 | convolution fusion | flops 571760640 | bytes 7028736 | tf_op jit(solution)/shard_map/kijc,kcd->ijd/dot_general | solution.py:162
  155.6 5.3 %all-to-all-start.2 = ((bf16[16,90,256]{2,1,0:T(8,128)(2,1)}), bf16[16,90,256]{2,1,0:T(8,128)(2,1)}, u32[]{:S(2)}, u32[]{:S(2)}) async-start(bf16[16,90,256]{2,1,0:T(8,128)(2,1)} %get-tuple-element.34), calls=%async_computation.2 | async-start | bytes 1572864 | tf_op jit(solution)/shard_map/all_to_all | solution.py:174
  160.9 2.4 convolution_convert_fusion
  166.1 6.0 %collective-permute-start.5 = (bf16[3,1,90,256]{3,2,0,1:T(8,128)(2,1)S(1)}, bf16[3,1,90,256]{3,2,0,1:T(8,128)(2,1)S(1)}, u32[]{:S(2)}, u32[]{:S(2)}) collective-permute-start(bf16[3,1,90,256]{3,2,0,1:T(8,128)(2,1)S(1)} %get-tuple-element.33), channel_id=1, source_target_pairs={{16,0},{32,16},{48,32},{64,48},{80,64},{96,80},{112,96},{128,112},... | collective-permute-start | bytes 414728 | tf_op jit(solution)/shard_map/ppermute | solution.py:17
  177.6 2.6 collective-permute-start.7
  183.8 3.8 fusion.19
  192.4 14.2 %copy.90 = bf16[1,1440,256]{2,0,1:T(2,128)(2,1)S(1)} copy(bf16[1,1440,256]{2,1,0:T(8,128)(2,1)S(1)} %fusion.23) | data formatting | bytes 1474560 | tf_op jit(solution)/shard_map/convert_element_type | solution.py:137
  206.6 7.8 %reduce.5 = bf16[1440,256]{1,0:T(8,128)(2,1)S(1)} reduce(bf16[1440,1,256]{2,1,0:T(2,128)(2,1)S(1)} %bitcast.124, bf16[]{:T(256)} %broadcast.75), dimensions={1}, to_apply=%bitcast.121.reduce_sub_computation | reduce | bytes 1474562
  215.5 5.4 %all-to-all-start.3 = ((bf16[16,2,11520]{2,1,0:T(2,128)(2,1)}), bf16[16,2,11520]{2,1,0:T(2,128)(2,1)}, u32[]{:S(2)}, u32[]{:S(2)}) async-start(bf16[16,2,11520]{2,1,0:T(2,128)(2,1)} %reshape.161), calls=%async_computation.3 | async-start | bytes 1474560 | tf_op jit(solution)/shard_map/all_to_all | solution.py:178
  221.3 3.5 convolution_bitcast_fusion
  231.5 3.1 fusion.10
  234.7 6.2 %all-to-all-done.3 = bf16[16,2,11520]{2,1,0:T(2,128)(2,1)} async-done(((bf16[16,2,11520]{2,1,0:T(2,128)(2,1)}), bf16[16,2,11520]{2,1,0:T(2,128)(2,1)}, u32[]{:S(2)}, u32[]{:S(2)}) %all-to-all-start.3) | async-done | bytes 737312 | tf_op jit(solution)/shard_map/all_to_all | solution.py:178
  240.9 5.1 %reshape.162 = bf16[1440,1,256]{2,1,0:T(2,128)(2,1)} reshape(bf16[16,2,11520]{2,1,0:T(2,128)(2,1)} %all-to-all-done.3) | data formatting | bytes 1474560
  246.0 9.9 %convert_reduce_fusion = f32[1440,256]{1,0:T(8,128)} fusion(bf16[1440,1,256]{2,1,0:T(2,128)(2,1)} %reshape.162), kind=kLoop, calls=%fused_computation.52 | loop fusion | flops 368640 | bytes 2211840 | tf_op jit(solution)/shard_map/convert_element_type | solution.py:187
  255.9 2.5 reshape.142
  258.5 3.8 fusion.31
  263.6 232.0 %all-reduce.4.cloned.1.call-done = (f32[3,256,256]{2,1,0:T(8,128)}, f32[2,720,256]{2,1,0:T(8,128)}) async-done(((f32[3,256,256]{2,1,0:T(8,128)}, f32[2,720,256]{2,1,0:T(8,128)}), (f32[3,256,256]{2,1,0:T(8,128)}, f32[2,720,256]{2,1,0:T(8,128)})) %all-reduce.4.cloned.1.call-update) | async-done | bytes 2261008 | tf_op jit(solution)/shard_map/psum | solution.py:179
  (109 shorter events, 48.6 us)
Async XLA Ops:
  7.2 143.1 %copy-start = (bf16[3,256,256]{2,1,0:T(8,128)(2,1)S(1)}, bf16[3,256,256]{2,1,0:T(8,128)(2,1)}, u32[]{:S(2)}) copy-start(bf16[3,256,256]{2,1,0:T(8,128)(2,1)} %param.10) | copy-start | bytes 1179652
  9.5 65.2 %all-to-all-start = ((bf16[16,90,256]{2,1,0:T(8,128)(2,1)}), bf16[16,90,256]{2,1,0:T(8,128)(2,1)S(1)}, u32[]{:S(2)}, u32[]{:S(2)}) async-start(bf16[16,90,256]{2,1,0:T(8,128)(2,1)} %copy.41), calls=%async_computation | async-start | bytes 1572864 | tf_op jit(solution)/shard_map/all_to_all | solution.py:165
  18.9 51.7 %collective-permute-start = (bf16[1,90,256]{2,1,0:T(8,128)(2,1)S(1)}, bf16[1,90,256]{2,1,0:T(8,128)(2,1)S(1)}, u32[]{:S(2)}, u32[]{:S(2)}) collective-permute-start(bf16[1,90,256]{2,1,0:T(8,128)(2,1)S(1)} %get-tuple-element.41), channel_id=1, source_target_pairs={{0,16},{16,32},{32,48},{48,64},{64,80},{80,96},{96,112},{112,128},... | collective-permute-start | bytes 138248 | tf_op jit(solution)/shard_map/ppermute | solution.py:16
  22.4 48.5 %collective-permute-start.1 = (bf16[1,90,256]{2,1,0:T(8,128)(2,1)S(1)}, bf16[1,90,256]{2,1,0:T(8,128)(2,1)S(1)}, u32[]{:S(2)}, u32[]{:S(2)}) collective-permute-start(bf16[1,90,256]{2,1,0:T(8,128)(2,1)S(1)} %get-tuple-element.40), channel_id=1, source_target_pairs={{16,0},{32,16},{48,32},{64,48},{80,64},{96,80},{112,96},{128,112},... | collective-permute-start | bytes 138248 | tf_op jit(solution)/shard_map/ppermute | solution.py:17
  26.9 20.0 %copy-start.26 = (bf16[3,256,3,33]{1,3,2,0:T(8,128)(2,1)S(1)}, bf16[3,256,3,33]{1,3,2,0:T(8,128)(2,1)}, u32[]{:S(2)}) copy-start(bf16[3,256,3,33]{1,3,2,0:T(8,128)(2,1)} %param.8) | copy-start | bytes 456196
  47.2 20.2 %copy-start.27 = (s32[256]{0:T(256)S(1)}, s32[256]{0:T(256)}, u32[]{:S(2)}) copy-start(s32[256]{0:T(256)} %param.9) | copy-start | bytes 3076
  68.7 1.9 copy-start.14
  71.7 41.3 %collective-permute-start.2 = (bf16[18,16,256]{2,1,0:T(8,128)(2,1)}, bf16[18,16,256]{2,1,0:T(8,128)(2,1)S(1)}, u32[]{:S(2)}, u32[]{:S(2)}) collective-permute-start(bf16[18,16,256]{2,1,0:T(8,128)(2,1)} %get-tuple-element.38), channel_id=1, source_target_pairs={{0,1},{1,2},{2,3},{3,4},{4,5},{5,6},{6,7},{7,8},{8,9},{9,10},{10,1... | collective-permute-start | bytes 442376 | tf_op jit(solution)/shard_map/ppermute | solution.py:16
  71.9 41.1 %collective-permute-start.3 = (bf16[18,16,256]{2,1,0:T(8,128)(2,1)}, bf16[18,16,256]{2,1,0:T(8,128)(2,1)}, u32[]{:S(2)}, u32[]{:S(2)}) collective-permute-start(bf16[18,16,256]{2,1,0:T(8,128)(2,1)} %get-tuple-element.39), channel_id=1, source_target_pairs={{1,0},{2,1},{3,2},{4,3},{5,4},{6,5},{7,6},{8,7},{9,8},{10,9},{11,1... | collective-permute-start | bytes 442376 | tf_op jit(solution)/shard_map/ppermute | solution.py:17
  75.7 3.9 copy-start.4
  75.8 4.2 copy-start.16
  105.8 27.1 %all-to-all-start.1 = ((bf16[16,2,11520]{2,1,0:T(2,128)(2,1)}), bf16[16,2,11520]{2,1,0:T(2,128)(2,1)}, u32[]{:S(2)}, u32[]{:S(2)}) async-start(bf16[16,2,11520]{2,1,0:T(2,128)(2,1)} %reshape.159), calls=%async_computation.1 | async-start | bytes 1474560 | tf_op jit(solution)/shard_map/all_to_all | solution.py:167
  155.6 26.2 %all-to-all-start.2 = ((bf16[16,90,256]{2,1,0:T(8,128)(2,1)}), bf16[16,90,256]{2,1,0:T(8,128)(2,1)}, u32[]{:S(2)}, u32[]{:S(2)}) async-start(bf16[16,90,256]{2,1,0:T(8,128)(2,1)} %get-tuple-element.34), calls=%async_computation.2 | async-start | bytes 1572864 | tf_op jit(solution)/shard_map/all_to_all | solution.py:174
  160.9 2.5 copy-start.10
  164.1 12.0 %copy-start.2 = (bf16[3,16,90,256]{3,2,0,1:T(8,128)(2,1)}, bf16[3,16,90,256]{3,2,0,1:T(8,128)(2,1)S(1)}, u32[]{:S(2)}) copy-start(bf16[3,16,90,256]{3,2,0,1:T(8,128)(2,1)S(1)} %convert_bitcast_fusion) | copy-start | bytes 6635524
  164.2 10.3 %collective-permute-start.4 = (bf16[3,1,90,256]{3,2,0,1:T(8,128)(2,1)S(1)}, bf16[3,1,90,256]{3,2,0,1:T(8,128)(2,1)S(1)}, u32[]{:S(2)}, u32[]{:S(2)}) collective-permute-start(bf16[3,1,90,256]{3,2,0,1:T(8,128)(2,1)S(1)} %get-tuple-element.32), channel_id=1, source_target_pairs={{0,16},{16,32},{32,48},{48,64},{64,80},{80,96},{96,112},{112,128},... | collective-permute-start | bytes 414728 | tf_op jit(solution)/shard_map/ppermute | solution.py:16
  166.1 10.1 %collective-permute-start.5 = (bf16[3,1,90,256]{3,2,0,1:T(8,128)(2,1)S(1)}, bf16[3,1,90,256]{3,2,0,1:T(8,128)(2,1)S(1)}, u32[]{:S(2)}, u32[]{:S(2)}) collective-permute-start(bf16[3,1,90,256]{3,2,0,1:T(8,128)(2,1)S(1)} %get-tuple-element.33), channel_id=1, source_target_pairs={{16,0},{32,16},{48,32},{64,48},{80,64},{96,80},{112,96},{128,112},... | collective-permute-start | bytes 414728 | tf_op jit(solution)/shard_map/ppermute | solution.py:17
  174.5 2.8 copy-start.22
  177.3 48.8 %collective-permute-start.6 = (bf16[3,18,16,256]{3,2,0,1:T(8,128)(2,1)}, bf16[3,18,16,256]{3,2,0,1:T(8,128)(2,1)}, u32[]{:S(2)}, u32[]{:S(2)}) collective-permute-start(bf16[3,18,16,256]{3,2,0,1:T(8,128)(2,1)} %get-tuple-element.30), channel_id=1, source_target_pairs={{0,1},{1,2},{2,3},{3,4},{4,5},{5,6},{6,7},{7,8},{8,9},{9,10},{10,1... | collective-permute-start | bytes 1327112 | tf_op jit(solution)/shard_map/ppermute | solution.py:16
  177.6 48.5 %collective-permute-start.7 = (bf16[3,18,16,256]{3,2,0,1:T(8,128)(2,1)}, bf16[3,18,16,256]{3,2,0,1:T(8,128)(2,1)}, u32[]{:S(2)}, u32[]{:S(2)}) collective-permute-start(bf16[3,18,16,256]{3,2,0,1:T(8,128)(2,1)} %get-tuple-element.31), channel_id=1, source_target_pairs={{1,0},{2,1},{3,2},{4,3},{5,4},{6,5},{7,6},{8,7},{9,8},{10,9},{11,1... | collective-permute-start | bytes 1327112 | tf_op jit(solution)/shard_map/ppermute | solution.py:17
  187.6 2.2 copy-start.17
  187.6 2.8 copy-start.18
  206.6 14.6 %copy-start.11 = (bf16[16,90,256]{2,1,0:T(8,128)(2,1)S(1)}, bf16[16,90,256]{2,1,0:T(8,128)(2,1)}, u32[]{:S(2)}) copy-start(bf16[16,90,256]{2,1,0:T(8,128)(2,1)} %get-tuple-element.34) | copy-start | bytes 2211844
  215.5 25.5 %all-to-all-start.3 = ((bf16[16,2,11520]{2,1,0:T(2,128)(2,1)}), bf16[16,2,11520]{2,1,0:T(2,128)(2,1)}, u32[]{:S(2)}, u32[]{:S(2)}) async-start(bf16[16,2,11520]{2,1,0:T(2,128)(2,1)} %reshape.161), calls=%async_computation.3 | async-start | bytes 1474560 | tf_op jit(solution)/shard_map/all_to_all | solution.py:178
  220.9 3.9 copy-start.21
  220.9 274.7 %all-reduce.4.cloned.1.call-start = ((), (), s32[]{:S(2)}) async-start(), calls=%async_computation.4 | async-start | bytes 4521984 | tf_op jit(solution)/shard_map/psum | solution.py:179
  221.2 4.8 copy-start.3
  221.2 4.8 copy-start.23
  221.2 4.8 copy-start.25
  226.0 2.3 copy-start.6
  495.6 2.2 copy-start.20
  495.6 3.3 copy-start.1
  (9 other events, 12.7 us)
Sparse Core Ops, SparseCore 0:
  231.7 263.8 all-reduce.3
where the time goes:
time: 516 us; the launch traced here: 506 us
  waiting for transfers between devices  255 us (49%)
  other arithmetic  85.3 us (17%)
  local copies, waits for them, and re-layouts  65.1 us (13%)
  starting transfers between devices  48.4 us (9%)
  matrix products  37.3 us (7%)
  between operations  15 us (3%)
    psum x1, waiting for transfers between devices, on_device(): grad_weight, grad_filter = lax.psum((mix_part, filter_part), ('lat', 'lon'))  232 us
    another operation x2, other arithmetic  40.2 us
    unnamed x69, local copies, waits for them, and re-layouts  27.5 us
    unnamed x2, other arithmetic  17.5 us
    ppermute x4, starting transfers between devices, extended(): after = lax.ppermute(initial, axis, down)  15.9 us
    convert_element_type x1, local copies, waits for them, and re-layouts, adjoint_modes(): spectral_grad = jnp.einsum('mn,imc->inc', forward_table, back_modes, pref...  14.2 us
    all_to_all x1, waiting for transfers between devices, on_device(): lax.all_to_all(from_modes(inverse_table, filtered), 'lon', split_axis=1,...  13.5 us
  transfers between devices with their start and end apart: 13, of which 5 were waited for; matrix products, arithmetic and copies ran while one was open for 31% of the time, Pallas kernels for 0%

commit v1 on v0

--- a/solution.py
+++ b/solution.py
@@ -2,6 +2,8 @@
 
 import jax
 import jax.numpy as jnp
+import ml_dtypes
+import numpy as np
 from jax import lax
 from jax.sharding import PartitionSpec as P
 
@@ -40,18 +42,25 @@
 
 
 def dft_tables(longitudes, wavenumbers):
-    cell_index = jnp.arange(longitudes, dtype=jnp.int32)
-    wave_index = jnp.arange(wavenumbers, dtype=jnp.int32)
+    cell_index = np.arange(longitudes, dtype=np.int64)
+    wave_index = np.arange(wavenumbers, dtype=np.int64)
     phase_index = wave_index[:, None] * cell_index[None, :] % longitudes
-    angles = phase_index.astype(jnp.float32) * (2.0 * math.pi / longitudes)
-    cosine_wave = jnp.cos(angles)
-    sine_wave = jnp.sin(angles)
-    forward_table = jnp.concatenate([cosine_wave, -sine_wave], axis=0).astype(jnp.bfloat16)
-    factor = jnp.where(wave_index == 0, 1.0, 2.0).astype(jnp.float32) / longitudes
-    inverse_table = jnp.concatenate(
+    angles = phase_index.astype(np.float32) * np.float32(2.0 * math.pi / longitudes)
+    cosine_wave = np.cos(angles)
+    sine_wave = np.sin(angles)
+    forward_table = np.concatenate([cosine_wave, -sine_wave], axis=0).astype(ml_dtypes.bfloat16)
+    factor = np.where(wave_index == 0, 1.0, 2.0).astype(np.float32) / np.float32(longitudes)
+    inverse_table = np.concatenate(
         [cosine_wave * factor[:, None], -sine_wave * factor[:, None]], axis=0
-    ).T.astype(jnp.bfloat16)
-    return (forward_table, inverse_table)
+    ).T.astype(ml_dtypes.bfloat16)
+    return (jnp.asarray(forward_table), jnp.asarray(np.ascontiguousarray(inverse_table)))
+
+
+def total(value):
+    flat = value.reshape(-1, value.shape[-1])
+    part = lax.psum_scatter(flat, "lat", scatter_dimension=0, tiled=True)
+    part = lax.psum(part, "lon")
+    return lax.all_gather(part, "lat", axis=0, tiled=True).reshape(value.shape)
 
 
 def silu_slope(values):
@@ -176,7 +185,7 @@
         forward_table, inverse_table, cot_field, spectrum, spectral_filter
     )
     spectral_grad = lax.all_to_all(owner_grad, "lon", split_axis=1, concat_axis=0, tiled=True)
-    grad_weight, grad_filter = lax.psum((mix_part, filter_part), ("lat", "lon"))
+    grad_weight, grad_filter = (total(mix_part), total(filter_part))
     products = jnp.einsum(
         "ijd,kcd->kijc", pre_grad, mix_weight, preferred_element_type=jnp.float32
     ).astype(jnp.bfloat16)

time: 516 us -> 467 us (0.905)
  blocking collectives: 0 us -> 152 us
  waiting for transfers between devices: 255 us -> 105 us
  other arithmetic: 85.3 us -> 39.9 us
    psum x1, waiting for transfers between devices: 232 us -> 82 us  [total(): part = lax.psum(part, 'lon')]
    psum x0 -> x1, blocking collectives: none -> 53.7 us  [total(): part = lax.psum(part, 'lon')]
    unnamed x0 -> x1, blocking collectives: none -> 45.7 us
    another operation x2 -> x0, other arithmetic: 40.2 us -> none
    all_to_all x0 -> x1, blocking collectives: none -> 27 us  [on_device(): lax.all_to_all(pre_grad, 'lon', split_axis=0, concat_axis=1, tiled=True)]
    all_gather x0 -> x1, blocking collectives: none -> 26 us  [total(): return lax.all_gather(part, 'lat', axis=0, tiled=True).reshape(value.shape)]
    all_to_all x1, waiting for transfers between devices: 6.23 us -> 0.01 us  [on_device(): lax.all_to_all(owner_grad, 'lon', split_axis=1, concat_axis=0, tiled=True)]
    all_to_all x1 -> x0, starting transfers between devices: 5.25 us -> none  [on_device(): lax.all_to_all(pre_grad, 'lon', split_axis=0, concat_axis=1, tiled=True)]
  transfers between devices with their start and end apart: 13 -> 15, of which waited for: 5 -> 4; matrix products, arithmetic and copies ran while one was open for 31% -> 22% of each run, Pallas kernels for 0% -> 0%
where the time goes in v1:
time: 467 us; the launch traced here: 459 us
  blocking collectives  152 us (33%)
  waiting for transfers between devices  105 us (22%)
  local copies, waits for them, and re-layouts  62.7 us (13%)
  starting transfers between devices  45.1 us (10%)
  other arithmetic  39.9 us (9%)
  matrix products  36.2 us (8%)
  between operations  17.2 us (4%)
    psum x1, waiting for transfers between devices, total(): part = lax.psum(part, 'lon')  82 us
    psum x1, blocking collectives, total(): part = lax.psum(part, 'lon')  53.7 us
    unnamed x1, blocking collectives  45.7 us
    all_to_all x1, blocking collectives, on_device(): lax.all_to_all(pre_grad, 'lon', split_axis=0, concat_axis=1, tiled=True)  27 us
    all_gather x1, blocking collectives, total(): return lax.all_gather(part, 'lat', axis=0, tiled=True).reshape(value.shape)  26 us
    unnamed x72, local copies, waits for them, and re-layouts  25.3 us
    unnamed x2, other arithmetic  17.1 us
    ppermute x4, starting transfers between devices, extended(): after = lax.ppermute(initial, axis, down)  16.3 us
  transfers between devices with their start and end apart: 15, of which 4 were waited for; matrix products, arithmetic and copies ran while one was open for 22% of the time, Pallas kernels for 0%

profile of v1, /device:TPU:2, one launch (start us, length us, event | category | flops | bytes accessed | tf_op | source)
XLA Modules:
  0.0 458.7 jit_solution(157500648997667569)
XLA Ops:
  10.3 8.7 %all-to-all-start = ((bf16[16,90,256]{2,1,0:T(8,128)(2,1)}), bf16[16,90,256]{2,1,0:T(8,128)(2,1)S(1)}, u32[]{:S(2)}, u32[]{:S(2)}) async-start(bf16[16,90,256]{2,1,0:T(8,128)(2,1)} %copy.43), calls=%async_computation | async-start | bytes 1572864 | tf_op jit(solution)/shard_map/all_to_all | solution.py:174
  19.9 3.5 collective-permute-start
  23.4 4.5 collective-permute-start.1
  32.7 2.8 collective-permute-start.3
  35.5 5.0 %all-to-all-done = bf16[16,90,256]{2,1,0:T(8,128)(2,1)S(1)} async-done(((bf16[16,90,256]{2,1,0:T(8,128)(2,1)}), bf16[16,90,256]{2,1,0:T(8,128)(2,1)S(1)}, u32[]{:S(2)}, u32[]{:S(2)}) %all-to-all-start) | async-done | bytes 737312 | tf_op jit(solution)/shard_map/all_to_all | solution.py:174
  40.7 3.7 convolution_bitcast_fusion.1
  46.9 14.2 %copy.93 = bf16[1,1440,256]{2,0,1:T(2,128)(2,1)S(1)} copy(bf16[1,1440,256]{2,1,0:T(8,128)(2,1)S(1)} %fusion.9) | data formatting | bytes 1474560 | tf_op jit(solution)/shard_map/convert_element_type | solution.py:120
  61.7 8.5 %reduce.4 = bf16[1440,256]{1,0:T(8,128)(2,1)} reduce(bf16[1440,1,256]{2,1,0:T(2,128)(2,1)S(1)} %bitcast.140, bf16[]{:T(256)} %broadcast.56), dimensions={1}, to_apply=%bitcast.139.reduce_sub_computation | reduce | bytes 1474562
  70.2 2.9 reshape.173
  73.1 5.0 %all-to-all-start.1 = ((bf16[16,2,11520]{2,1,0:T(2,128)(2,1)}), bf16[16,2,11520]{2,1,0:T(2,128)(2,1)}, u32[]{:S(2)}, u32[]{:S(2)}) async-start(bf16[16,2,11520]{2,1,0:T(2,128)(2,1)} %reshape.173), calls=%async_computation.1 | async-start | bytes 1474560 | tf_op jit(solution)/shard_map/all_to_all | solution.py:176
  84.4 13.6 %all-to-all-done.1 = bf16[16,2,11520]{2,1,0:T(2,128)(2,1)} async-done(((bf16[16,2,11520]{2,1,0:T(2,128)(2,1)}), bf16[16,2,11520]{2,1,0:T(2,128)(2,1)}, u32[]{:S(2)}, u32[]{:S(2)}) %all-to-all-start.1) | async-done | bytes 737312 | tf_op jit(solution)/shard_map/all_to_all | solution.py:176
  98.1 4.2 reshape.174
  102.3 8.8 %convert_reduce_fusion.1 = f32[1440,256]{1,0:T(8,128)} fusion(bf16[1440,1,256]{2,1,0:T(2,128)(2,1)S(1)} %reshape.174), kind=kLoop, calls=%fused_computation.36 | loop fusion | flops 368640 | bytes 2211840 | tf_op jit(solution)/shard_map/convert_element_type | solution.py:179
  113.7 4.8 %fusion.16 = (bf16[16,90,256]{2,1,0:T(8,128)(2,1)S(1)}, bf16[16,90,256]{2,1,0:T(8,128)(2,1)}) fusion(bf16[16,90,256]{2,0,1:T(8,128)(2,1)} %param.9, bf16[16,90,256]{2,0,1:T(8,128)(2,1)S(1)} %copy-done.16, f32[16,90,256]{2,1,0:T(8,128)} %reshape.151, bf16[3,16,90,256]{3,2,0,1:T(8,128)(2,1)} %fusion.11, bf16[3,256,256]{2,1,0:T(8,128)(2,1)S(1)} %copy-done), kind=kOutput, calls=%fused_computation.26 | convolution fusion | flops 571760640 | bytes 7028736 | tf_op jit(solution)/shard_map/kijc,kcd->ijd/dot_general | solution.py:171
  118.5 27.0 %all_to_all.16 = bf16[16,90,256]{2,1,0:T(8,128)(2,1)S(1)} all-to-all(bf16[16,90,256]{2,1,0:T(8,128)(2,1)S(1)} %get-tuple-element.28), channel_id=1, replica_groups=mesh['lat'=16,'lon'=16] {'lon'}, dimensions={0} | all-to-all | bytes 1474560 | tf_op jit(solution)/shard_map/all_to_all | solution.py:183
  146.5 4.4 convolution_bitcast_fusion
  152.2 45.7 %fusion = f32[96,256]{1,0:T(8,128)S(1)} fusion(f32[1440,256]{1,0:T(8,128)S(1)} %bitcast.141), kind=kCustom, calls=%all-reduce-scatter | all-reduce-scatter fusion | flops 393217 | bytes 1573888
  197.9 2.8 collective-permute-start.8
  202.0 4.5 collective-permute-done.8
  207.7 3.4 fusion.31
  215.4 6.2 %collective-permute-start.5 = (bf16[3,1,90,256]{3,2,0,1:T(8,128)(2,1)S(1)}, bf16[3,1,90,256]{3,2,0,1:T(8,128)(2,1)S(1)}, u32[]{:S(2)}, u32[]{:S(2)}) collective-permute-start(bf16[3,1,90,256]{3,2,0,1:T(8,128)(2,1)S(1)} %get-tuple-element.27), channel_id=1, source_target_pairs={{16,0},{32,16},{48,32},{64,48},{80,64},{96,80},{112,96},{128,112},... | collective-permute-start | bytes 414728 | tf_op jit(solution)/shard_map/ppermute | solution.py:19
  226.4 2.9 collective-permute-start.7
  229.3 82.0 %all-reduce.5.cloned.1.call-done = f32[90,256]{1,0:T(8,128)} async-done(((f32[90,256]{1,0:T(8,128)}), f32[90,256]{1,0:T(8,128)}) %all-reduce.5.cloned.1.call-update) | async-done | bytes 92176 | tf_op jit(solution)/shard_map/psum | solution.py:62
  311.4 3.7 fusion.42
  316.5 9.3 %copy.92 = bf16[1,1440,256]{2,0,1:T(2,128)(2,1)} copy(bf16[1,1440,256]{2,1,0:T(8,128)(2,1)S(1)} %fusion.10) | data formatting | bytes 1474560 | tf_op jit(solution)/shard_map/convert_element_type | solution.py:146
  325.8 8.6 %reduce.5 = bf16[1440,256]{1,0:T(8,128)(2,1)S(1)} reduce(bf16[1440,1,256]{2,1,0:T(2,128)(2,1)} %bitcast.142, bf16[]{:T(256)} %broadcast.56), dimensions={1}, to_apply=%bitcast.138.reduce_sub_computation | reduce | bytes 1474562
  335.5 6.3 %all-to-all-start.3 = ((bf16[16,2,11520]{2,1,0:T(2,128)(2,1)}), bf16[16,2,11520]{2,1,0:T(2,128)(2,1)}, u32[]{:S(2)}, u32[]{:S(2)}) async-start(bf16[16,2,11520]{2,1,0:T(2,128)(2,1)} %reshape.175), calls=%async_computation.3 | async-start | bytes 1474560 | tf_op jit(solution)/shard_map/all_to_all | solution.py:187
  348.2 53.7 %psum.14 = f32[48,256]{1,0:T(8,128)S(1)} all-reduce(f32[48,256]{1,0:T(8,128)} %reduce-scatter.4.cloned.1.call-done), channel_id=1, replica_groups=mesh['lat'=16,'lon'=16] {'lon'}, use_global_device_ids=true, to_apply=%region_1.2 | all-reduce | flops 12288 | bytes 98304 | tf_op jit(solution)/shard_map/psum | solution.py:62
  401.8 26.0 %all_gather.6 = f32[768,256]{1,0:T(8,128)} all-gather(f32[48,256]{1,0:T(8,128)S(1)} %psum.14), channel_id=1, replica_groups=mesh['lat'=16,'lon'=16] {'lat'}, dimensions={0}, use_global_device_ids=true | all-gather | bytes 835584 | tf_op jit(solution)/shard_map/all_gather | solution.py:63
  427.8 4.2 reshape.176
  432.1 8.8 %convert_reduce_fusion = f32[1440,256]{1,0:T(8,128)} fusion(bf16[1440,1,256]{2,1,0:T(2,128)(2,1)S(1)} %reshape.176), kind=kLoop, calls=%fused_computation.35 | loop fusion | flops 368640 | bytes 2211840 | tf_op jit(solution)/shard_map/convert_element_type | solution.py:196
  442.3 3.8 fusion.18
  (121 shorter events, 48.1 us)
Async XLA Ops:
  8.0 105.7 %copy-start = (bf16[3,256,256]{2,1,0:T(8,128)(2,1)S(1)}, bf16[3,256,256]{2,1,0:T(8,128)(2,1)}, u32[]{:S(2)}) copy-start(bf16[3,256,256]{2,1,0:T(8,128)(2,1)} %param.12) | copy-start | bytes 1179652
  8.0 19.9 %copy-start.25 = (bf16[3,256,3,33]{1,3,2,0:T(8,128)(2,1)S(1)}, bf16[3,256,3,33]{1,3,2,0:T(8,128)(2,1)}, u32[]{:S(2)}) copy-start(bf16[3,256,3,33]{1,3,2,0:T(8,128)(2,1)} %param.10) | copy-start | bytes 456196
  10.3 17.9 %copy-start.26 = (s32[256]{0:T(256)S(1)}, s32[256]{0:T(256)}, u32[]{:S(2)}) copy-start(s32[256]{0:T(256)} %param.11) | copy-start | bytes 3076
  10.3 30.2 %all-to-all-start = ((bf16[16,90,256]{2,1,0:T(8,128)(2,1)}), bf16[16,90,256]{2,1,0:T(8,128)(2,1)S(1)}, u32[]{:S(2)}, u32[]{:S(2)}) async-start(bf16[16,90,256]{2,1,0:T(8,128)(2,1)} %copy.43), calls=%async_computation | async-start | bytes 1572864 | tf_op jit(solution)/shard_map/all_to_all | solution.py:174
  19.9 11.5 %collective-permute-start = (bf16[1,90,256]{2,1,0:T(8,128)(2,1)S(1)}, bf16[1,90,256]{2,1,0:T(8,128)(2,1)S(1)}, u32[]{:S(2)}, u32[]{:S(2)}) collective-permute-start(bf16[1,90,256]{2,1,0:T(8,128)(2,1)S(1)} %get-tuple-element.33), channel_id=1, source_target_pairs={{0,16},{16,32},{32,48},{48,64},{64,80},{80,96},{96,112},{112,128},... | collective-permute-start | bytes 138248 | tf_op jit(solution)/shard_map/ppermute | solution.py:18
  23.4 8.3 %collective-permute-start.1 = (bf16[1,90,256]{2,1,0:T(8,128)(2,1)S(1)}, bf16[1,90,256]{2,1,0:T(8,128)(2,1)S(1)}, u32[]{:S(2)}, u32[]{:S(2)}) collective-permute-start(bf16[1,90,256]{2,1,0:T(8,128)(2,1)S(1)} %get-tuple-element.32), channel_id=1, source_target_pairs={{16,0},{32,16},{48,32},{64,48},{80,64},{96,80},{112,96},{128,112},... | collective-permute-start | bytes 138248 | tf_op jit(solution)/shard_map/ppermute | solution.py:19
  32.5 45.7 %collective-permute-start.2 = (bf16[18,16,256]{2,1,0:T(8,128)(2,1)}, bf16[18,16,256]{2,1,0:T(8,128)(2,1)S(1)}, u32[]{:S(2)}, u32[]{:S(2)}) collective-permute-start(bf16[18,16,256]{2,1,0:T(8,128)(2,1)} %get-tuple-element.30), channel_id=1, source_target_pairs={{0,1},{1,2},{2,3},{3,4},{4,5},{5,6},{6,7},{7,8},{8,9},{9,10},{10,1... | collective-permute-start | bytes 442376 | tf_op jit(solution)/shard_map/ppermute | solution.py:18
  32.7 45.5 %collective-permute-start.3 = (bf16[18,16,256]{2,1,0:T(8,128)(2,1)}, bf16[18,16,256]{2,1,0:T(8,128)(2,1)}, u32[]{:S(2)}, u32[]{:S(2)}) collective-permute-start(bf16[18,16,256]{2,1,0:T(8,128)(2,1)} %get-tuple-element.31), channel_id=1, source_target_pairs={{1,0},{2,1},{3,2},{4,3},{5,4},{6,5},{7,6},{8,7},{9,8},{10,9},{11,1... | collective-permute-start | bytes 442376 | tf_op jit(solution)/shard_map/ppermute | solution.py:19
  40.7 3.7 copy-start.2
  40.7 3.7 copy-start.6
  73.1 6.6 %copy-start.11 = (bf16[3,16,122,90]{2,1,3,0:T(8,128)(2,1)S(1)}, bf16[3,16,122,90]{2,1,3,0:T(8,128)(2,1)}, u32[]{:S(2)}) copy-start(bf16[3,16,122,90]{2,1,3,0:T(8,128)(2,1)} %get-tuple-element.20) | copy-start | bytes 3162244
  73.1 25.0 %all-to-all-start.1 = ((bf16[16,2,11520]{2,1,0:T(2,128)(2,1)}), bf16[16,2,11520]{2,1,0:T(2,128)(2,1)}, u32[]{:S(2)}, u32[]{:S(2)}) async-start(bf16[16,2,11520]{2,1,0:T(2,128)(2,1)} %reshape.173), calls=%async_computation.1 | async-start | bytes 1474560 | tf_op jit(solution)/shard_map/all_to_all | solution.py:176
  78.0 233.2 %all-reduce.5.cloned.1.call-start = ((), (), s32[]{:S(2)}) async-start(), calls=%async_computation.6 | async-start | bytes 196608 | tf_op jit(solution)/shard_map/psum | solution.py:62
  111.0 2.6 copy-start.16
  152.2 48.5 %copy-start.27 = (u32[256]{0:T(256)S(1)}, u32[256]{0:T(256)}, u32[]{:S(2)}) copy-start(u32[256]{0:T(256)} %constant.40) | copy-start | bytes 3076
  197.9 8.6 %collective-permute-start.8 = (f32[90,256]{1,0:T(8,128)S(1)}, f32[90,256]{1,0:T(8,128)S(1)}, u32[]{:S(2)}, u32[]{:S(2)}) collective-permute-start(f32[90,256]{1,0:T(8,128)S(1)} %slice.138), channel_id=1, source_target_pairs={{0,16},{16,32},{32,48},{48,64},{64,80},{80,96},{96,112},{112,128},... | collective-permute-start | bytes 276488
  207.4 3.7 copy-start.8
  207.5 140.7 %reduce-scatter.4.cloned.1.call-start = ((), (), s32[]{:S(2)}) async-start(), calls=%async_computation.5 | async-start | bytes 835584 | tf_op jit(solution)/shard_map/reduce_scatter | solution.py:61
  211.1 236.3 %all-gather.3.cloned.1.call-start = ((), (), s32[]{:S(2)}) async-start(), calls=%async_computation.7 | async-start | bytes 1671168 | tf_op jit(solution)/shard_map/all_gather | solution.py:63
  213.5 11.8 %collective-permute-start.4 = (bf16[3,1,90,256]{3,2,0,1:T(8,128)(2,1)S(1)}, bf16[3,1,90,256]{3,2,0,1:T(8,128)(2,1)S(1)}, u32[]{:S(2)}, u32[]{:S(2)}) collective-permute-start(bf16[3,1,90,256]{3,2,0,1:T(8,128)(2,1)S(1)} %get-tuple-element.26), channel_id=1, source_target_pairs={{0,16},{16,32},{32,48},{48,64},{64,80},{80,96},{96,112},{112,128},... | collective-permute-start | bytes 414728 | tf_op jit(solution)/shard_map/ppermute | solution.py:18
  215.4 8.5 %copy-start.20 = (bf16[16,90,256]{2,1,0:T(8,128)(2,1)S(1)}, bf16[16,90,256]{2,1,0:T(8,128)(2,1)}, u32[]{:S(2)}) copy-start(bf16[16,90,256]{2,1,0:T(8,128)(2,1)} %get-tuple-element.29) | copy-start | bytes 2211844
  215.4 9.8 %collective-permute-start.5 = (bf16[3,1,90,256]{3,2,0,1:T(8,128)(2,1)S(1)}, bf16[3,1,90,256]{3,2,0,1:T(8,128)(2,1)S(1)}, u32[]{:S(2)}, u32[]{:S(2)}) collective-permute-start(bf16[3,1,90,256]{3,2,0,1:T(8,128)(2,1)S(1)} %get-tuple-element.27), channel_id=1, source_target_pairs={{16,0},{32,16},{48,32},{64,48},{80,64},{96,80},{112,96},{128,112},... | collective-permute-start | bytes 414728 | tf_op jit(solution)/shard_map/ppermute | solution.py:19
  226.4 115.5 %collective-permute-start.6 = (bf16[3,18,16,256]{3,2,0,1:T(8,128)(2,1)}, bf16[3,18,16,256]{3,2,0,1:T(8,128)(2,1)}, u32[]{:S(2)}, u32[]{:S(2)}) collective-permute-start(bf16[3,18,16,256]{3,2,0,1:T(8,128)(2,1)} %get-tuple-element.24), channel_id=1, source_target_pairs={{0,1},{1,2},{2,3},{3,4},{4,5},{5,6},{6,7},{7,8},{8,9},{9,10},{10,1... | collective-permute-start | bytes 1327112 | tf_op jit(solution)/shard_map/ppermute | solution.py:18
  226.4 115.5 %collective-permute-start.7 = (bf16[3,18,16,256]{3,2,0,1:T(8,128)(2,1)}, bf16[3,18,16,256]{3,2,0,1:T(8,128)(2,1)}, u32[]{:S(2)}, u32[]{:S(2)}) collective-permute-start(bf16[3,18,16,256]{3,2,0,1:T(8,128)(2,1)} %get-tuple-element.25), channel_id=1, source_target_pairs={{1,0},{2,1},{3,2},{4,3},{5,4},{6,5},{7,6},{8,7},{9,8},{10,9},{11,1... | collective-permute-start | bytes 1327112 | tf_op jit(solution)/shard_map/ppermute | solution.py:19
  311.3 3.7 copy-start.3
  311.3 3.7 copy-start.5
  311.3 4.0 copy-start.17
  335.5 6.4 %copy-start.22 = (bf16[3,1,90,256]{3,2,0,1:T(8,128)(2,1)S(1)}, bf16[3,1,90,256]{3,2,0,1:T(8,128)(2,1)}, u32[]{:S(2)}) copy-start(bf16[3,1,90,256]{3,2,0,1:T(8,128)(2,1)} %copy-done.21) | copy-start | bytes 414724
  335.5 6.4 %copy-start.24 = (bf16[3,1,90,256]{3,2,0,1:T(8,128)(2,1)S(1)}, bf16[3,1,90,256]{3,2,0,1:T(8,128)(2,1)}, u32[]{:S(2)}) copy-start(bf16[3,1,90,256]{3,2,0,1:T(8,128)(2,1)} %copy-done.23) | copy-start | bytes 414724
  335.5 92.4 %all-to-all-start.3 = ((bf16[16,2,11520]{2,1,0:T(2,128)(2,1)}), bf16[16,2,11520]{2,1,0:T(2,128)(2,1)}, u32[]{:S(2)}, u32[]{:S(2)}) async-start(bf16[16,2,11520]{2,1,0:T(2,128)(2,1)} %reshape.175), calls=%async_computation.3 | async-start | bytes 1474560 | tf_op jit(solution)/shard_map/all_to_all | solution.py:187
  341.8 2.3 copy-start.13
  447.4 2.6 copy-start.14
  (11 other events, 15.3 us)
Sparse Core Ops, SparseCore 0:
  207.6 103.6 all-reduce.4
Sparse Core Ops, SparseCore 1:
  211.4 76.8 reduce-scatter.3
  311.4 49.1 all-gather.2

commit v2 on v1

v2 whole, which is shorter than its diff:
```python
import functools
import math

import jax
import jax.numpy as jnp
import ml_dtypes
import numpy as np
from jax import lax
from jax.experimental import pallas as pl
from jax.experimental.pallas import tpu as pltpu
from jax.sharding import PartitionSpec as P

MESH = pl.DeviceIdType.MESH
F32 = jnp.float32
BF16 = jnp.bfloat16

ROWS = 16
COLS = 90
PAD = 96
WAVES = 720
WAVES_PAD = 768
SPREAD = 16
LANES = 128
CHANNELS = 256
WIDE = 128
TILE = 384


def masked_basis(disco_basis, support_width):
    spread = disco_basis.shape[3] // 2
    offsets = jnp.abs(jnp.arange(2 * spread + 1, dtype=jnp.int32) - spread)
    retained = offsets[None, :] <= support_width[:, None]
    return jnp.where(retained[None, :, None, :], disco_basis, jnp.zeros_like(disco_basis))


def dft_tables():
    longitudes = ROWS * COLS
    cell_index = np.arange(longitudes, dtype=np.int64)
    wave_index = np.arange(WAVES, dtype=np.int64)
    phase_index = wave_index[:, None] * cell_index[None, :] % longitudes
    angles = phase_index.astype(np.float32) * np.float32(2.0 * math.pi / longitudes)
    cosine_wave = np.cos(angles)
    sine_wave = np.sin(angles)
    factor = np.where(wave_index == 0, 1.0, 2.0).astype(np.float32) / np.float32(longitudes)

    def padded(real, imag):
        table = np.zeros((2, WAVES_PAD, ROWS, PAD), np.float32)
        table[0, :WAVES, :, :COLS] = real.reshape(WAVES, ROWS, COLS)
        table[1, :WAVES, :, :COLS] = imag.reshape(WAVES, ROWS, COLS)
        return table.reshape(2 * WAVES_PAD, ROWS * PAD).astype(ml_dtypes.bfloat16)

    forward = padded(cosine_wave, -sine_wave)
    inverse_t = padded(cosine_wave * factor[:, None], -sine_wave * factor[:, None])
    return (
        forward,
        np.ascontiguousarray(inverse_t.T),
        inverse_t,
        np.ascontiguousarray(forward.T),
    )


def kernel(
    x_ref, ct_ref, vf_ref, vb_ref, mix_ref, sf_ref, t0_ref, t1_ref, t2_ref, t3_ref,
    out_ref, gin_ref, gw_ref, gf_ref,
    tables, cts, slab, pslab, tail, ptail, xs, g1, ys, s1, ps, g2, zs, s2,
    resp, dense, spectrum, cotspec, modes, band,
    ws, wr, w2s, w2r, w3, wfin, fs, fr, f2s, f2r, f3, ffin,
    table_sem, a_send, a_recv, halo_send, halo_recv, ar_send, ar_recv,
):
    me = lax.axis_index("lon")
    lat = lax.axis_index("lat")
    right = lax.rem(me + 1, ROWS)
    left = lax.rem(me + ROWS - 1, ROWS)

    table_copies = [
        pltpu.make_async_copy(ref, tables.at[i], table_sem.at[i])
        for i, ref in enumerate((t0_ref, t1_ref, t2_ref, t3_ref))
    ]
    for copy in table_copies:
        copy.start()

    barrier = pltpu.get_barrier_semaphore()

    def greet(step, carry):
        pl.semaphore_signal(
            barrier, inc=1, device_id={"lon": lax.rem(me + step, ROWS)}, device_id_type=MESH
        )
        pl.semaphore_signal(
            barrier, inc=1, device_id={"lat": lax.rem(lat + step, ROWS)}, device_id_type=MESH
        )
        return carry

    lax.fori_loop(1, ROWS, greet, 0)

    def pack(i, carry):
        slab[i + 1, 80:PAD, :] = jnp.zeros((PAD - 80, CHANNELS), BF16)
        slab[i + 1, 0:COLS, :] = x_ref[i]
        cts[i, 80:PAD, :] = jnp.zeros((PAD - 80, CHANNELS), BF16)
        cts[i, 0:COLS, :] = ct_ref[i]
        for h in range(2):
            xs[h, i] = slab[i + 1, 0:PAD, h * LANES : (h + 1) * LANES]
        return carry

    lax.fori_loop(0, ROWS, pack, 0)
    pl.semaphore_wait(barrier, 2 * (ROWS - 1))

    def offset(step):
        return 8 + (1 - 2 * lax.rem(step, 2)) * lax.div(step + 1, 2)

    def spread_start(source, target, h, phase):
        def body(step, carry):
            peer = lax.rem(me + offset(step), ROWS)
            pltpu.make_async_remote_copy(
                src_ref=source.at[h, peer],
                dst_ref=target.at[h, me],
                send_sem=a_send.at[phase, h],
                recv_sem=a_recv.at[phase, h],
                device_id={"lon": peer},
                device_id_type=MESH,
            ).start()
            return carry

        lax.fori_loop(0, ROWS - 1, body, 0)

    def own_piece(source, target, h):
        target[h, me] = source[h, me]

    def wait_bytes(ref, sem):
        pltpu.make_async_copy(ref, ref, sem).wait()

    def spread_wait(target, h, phase):
        wait_bytes(target.at[h, pl.ds(0, ROWS - 1)], a_recv.at[phase, h])

    def halo_copy(src, dst, index, device):
        return pltpu.make_async_remote_copy(
            src_ref=src,
            dst_ref=dst,
            send_sem=halo_send.at[index],
            recv_sem=halo_recv.at[index],
            device_id=device,
            device_id_type=MESH,
        )

    def lat_halo(buf, base):
        up = halo_copy(
            buf.at[1, pl.ds(0, PAD)], buf.at[17, pl.ds(0, PAD)], base, {"lat": lax.max(lat - 1, 0)}
        )
        down = halo_copy(
            buf.at[16, pl.ds(0, PAD)],
            buf.at[0, pl.ds(0, PAD)],
            base + 1,
            {"lat": lax.min(lat + 1, ROWS - 1)},
        )
        return up, down

    def lon_halo(buf, end, base):
        pairs = []
        for n, rows in enumerate((pl.ds(1, ROWS), pl.ds(0, 1), pl.ds(17, 1))):
            pairs.append(
                (
                    halo_copy(
                        buf.at[rows, pl.ds(0, SPREAD)],
                        buf.at[rows, pl.ds(PAD, SPREAD)],
                        base + 2 + 2 * n,
                        {"lon": left},
                    ),
                    halo_copy(
                        end.at[rows],
                        buf.at[rows, pl.ds(PAD + SPREAD, SPREAD)],
                        base + 3 + 2 * n,
                        {"lon": right},
                    ),
                )
            )
        return pairs

    def tail_row(buf, end, i):
        moved = pltpu.roll(buf[i, 0:PAD, :].astype(F32), PAD - COLS, 0)
        end[i] = moved[PAD - SPREAD : PAD].astype(BF16)

    def halo_begin(buf, end, base):
        up, down = lat_halo(buf, base)

        @pl.when(lat > 0)
        def _():
            up.start()

        @pl.when(lat < ROWS - 1)
        def _():
            down.start()

        def body(i, carry):
            tail_row(buf, end, i + 1)
            return carry

        lax.fori_loop(0, ROWS, body, 0)
        for copy in lon_halo(buf, end, base)[0]:
            copy.start()

    def halo_middle(buf, end, base):
        up, down = lat_halo(buf, base)

        @pl.when(lat > 0)
        def _():
            down.wait_recv()

        @pl.when(lat == 0)
        def _():
            buf[0, 0:PAD, :] = jnp.zeros((PAD, CHANNELS), BF16)

        @pl.when(lat < ROWS - 1)
        def _():
            up.wait_recv()

        @pl.when(lat == ROWS - 1)
        def _():
            buf[17, 0:PAD, :] = jnp.zeros((PAD, CHANNELS), BF16)

        tail_row(buf, end, 0)
        tail_row(buf, end, 17)
        for pair in lon_halo(buf, end, base)[1:]:
            for copy in pair:
                copy.start()

    def halo_wait(buf, end, base):
        for pair in lon_halo(buf, end, base):
            for copy in pair:
                copy.wait_recv()

    def halo_end(buf, end, base):
        up, down = lat_halo(buf, base)

        @pl.when(lat > 0)
        def _():
            up.wait_send()

        @pl.when(lat < ROWS - 1)
        def _():
            down.wait_send()

        for pair in lon_halo(buf, end, base):
            for copy in pair:
                copy.wait_send()

    lane = lax.broadcasted_iota(jnp.int32, (PAD, WIDE), 1)
    row = lax.broadcasted_iota(jnp.int32, (PAD, WIDE), 0)
    direct = (row < COLS) & ((lane < COLS) | (lane >= PAD + SPREAD))
    shifted = (row < COLS) & (lane >= PAD) & (lane < PAD + SPREAD)

    def apply_band(vec_ref, buf):
        def body(i, carry):
            for k in range(3):
                for r in range(3):
                    vec = jnp.broadcast_to(vec_ref[i, 3 * k + r : 3 * k + r + 1, :], (PAD, WIDE))
                    near = pltpu.roll(vec, 0, 1, stride=1, stride_axis=0)
                    far = pltpu.roll(vec, PAD - COLS, 1, stride=1, stride_axis=0)
                    part = jnp.where(direct, near, jnp.where(shifted, far, 0.0))
                    band[k * PAD : (k + 1) * PAD, r * WIDE : (r + 1) * WIDE] = part.astype(BF16)
            around = buf[pl.ds(i, 3)].reshape(3 * WIDE, CHANNELS)
            value = jnp.dot(band[...], around, preferred_element_type=F32).astype(BF16)
            for k in range(3):
                resp[k, i] = value[k * PAD : (k + 1) * PAD]
            return carry

        lax.fori_loop(0, ROWS, body, 0)

    def mix(transposed):
        def body(n, carry):
            total = jnp.zeros((TILE, CHANNELS), F32)
            for k in range(3):
                part = resp[k, pl.ds(4 * n, 4)].reshape(TILE, CHANNELS)
                total = total + lax.dot_general(
                    part,
                    mix_ref[k],
                    (((1,), (1 if transposed else 0,)), ((), ())),
                    preferred_element_type=F32,
                )
            dense[pl.ds(4 * n, 4)] = total.reshape(4, PAD, CHANNELS)
            return carry

        lax.fori_loop(0, 4, body, 0)

    def to_spectrum(table, field, h, target):
        def body(n, carry):
            rows = pl.ds(pl.multiple_of(n * TILE, TILE), TILE)
            target[rows, :] = jnp.dot(
                tables[table, rows, :],
                field[h].reshape(ROWS * PAD, LANES),
                preferred_element_type=F32,
            )
            return carry

        lax.fori_loop(0, 4, body, 0)

    def to_field(table, field, h):
        def body(n, carry):
            rows = pl.ds(pl.multiple_of(n * TILE, TILE), TILE)
            value = jnp.dot(tables[table, rows, :], modes[...], preferred_element_type=F32)
            field[h, pl.ds(4 * n, 4)] = value.astype(BF16).reshape(4, PAD, LANES)
            return carry

        lax.fori_loop(0, 4, body, 0)

    for h in range(2):
        spread_start(xs, g1, h, 0)
        own_piece(xs, g1, h)
    halo_begin(slab, tail, 0)
    halo_middle(slab, tail, 0)
    halo_wait(slab, tail, 0)
    apply_band(vf_ref, slab)
    mix(False)

    modes[WAVES:WAVES_PAD, :] = jnp.zeros((WAVES_PAD - WAVES, LANES), BF16)
    modes[WAVES_PAD + WAVES :, :] = jnp.zeros((WAVES_PAD - WAVES, LANES), BF16)
    STEP = 144
    for copy in table_copies:
        copy.wait()

    for h in range(2):
        lanes = slice(h * LANES, (h + 1) * LANES)
        spread_wait(g1, h, 0)
        to_spectrum(0, g1, h, spectrum.at[h])

        def gain(n, carry):
            low = pl.ds(pl.multiple_of(n * STEP, 16), STEP)
            high = pl.ds(pl.multiple_of(WAVES_PAD + n * STEP, 16), STEP)
            real_part, imag_part = spectrum[h, low, :], spectrum[h, high, :]
            real_gain, imag_gain = sf_ref[0, low, lanes], sf_ref[1, low, lanes]
            modes[low, :] = (real_gain * real_part - imag_gain * imag_part).astype(BF16)
            modes[high, :] = (real_gain * imag_part + imag_gain * real_part).astype(BF16)
            return carry

        lax.fori_loop(0, WAVES // STEP, gain, 0)
        to_field(1, ys, h)
        spread_start(ys, s1, h, 1)
        own_piece(ys, s1, h)

    for h in range(2):
        lanes = slice(h * LANES, (h + 1) * LANES)
        spread_wait(s1, h, 1)

        def activate(i, carry):
            preact = dense[i, :, lanes] + s1[h, i].astype(F32)
            logistic = 1.0 / (1.0 + jnp.exp(-preact))
            own = slab[i + 1, 0:PAD, lanes].astype(F32)
            out_ref[i, :, lanes] = (own + preact * logistic).astype(BF16)
            slope = logistic * (1.0 + preact * (1.0 - logistic))
            grad = (cts[i, :, lanes].astype(F32) * slope).astype(BF16)
            ps[h, i] = grad
            pslab[i + 1, 0:PAD, lanes] = grad
            return carry

        lax.fori_loop(0, ROWS, activate, 0)
        spread_start(ps, g2, h, 2)
        own_piece(ps, g2, h)

    halo_begin(pslab, ptail, 8)

    for k in range(3):
        total = jnp.zeros((CHANNELS, CHANNELS), F32)
        part = lax.dot_general(
            resp[k].reshape(ROWS * PAD, CHANNELS),
            pslab[1:17, 0:PAD, :].reshape(ROWS * PAD, CHANNELS),
            (((0,), (0,)), ((), ())),
            preferred_element_type=F32,
        )
        ws[16 * k : 16 * (k + 1)] = part.astype(BF16).reshape(16, 16, CHANNELS)

    def lat_spread(source, target, index):
        def body(step, carry):
            peer = lax.rem(lat + step, ROWS)
            pltpu.make_async_remote_copy(
                src_ref=source(peer),
                dst_ref=target,
                send_sem=ar_send.at[index],
                recv_sem=ar_recv.at[index],
                device_id={"lat": peer},
                device_id_type=MESH,
            ).start()
            return carry

        lax.fori_loop(1, ROWS, body, 0)

    lat_spread(lambda peer: ws.at[pl.ds(3 * peer, 3)], wr.at[lat], 0)
    wr[lat] = ws[pl.ds(3 * lat, 3)]
    halo_middle(pslab, ptail, 8)

    for h in range(2):
        lanes = slice(h * LANES, (h + 1) * LANES)
        spread_wait(g2, h, 2)
        cot_modes = cotspec
        to_spectrum(2, g2, h, cot_modes)
        fs[h, 45:48] = jnp.zeros((3, 16, LANES), BF16)
        fs[h, 93:96] = jnp.zeros((3, 16, LANES), BF16)

        def back(n, carry):
            low = pl.ds(pl.multiple_of(n * STEP, 16), STEP)
            high = pl.ds(pl.multiple_of(WAVES_PAD + n * STEP, 16), STEP)
            real_part, imag_part = spectrum[h, low, :], spectrum[h, high, :]
            real_cot, imag_cot = cot_modes[low, :], cot_modes[high, :]
            real_gain, imag_gain = sf_ref[0, low, lanes], sf_ref[1, low, lanes]
            modes[low, :] = (real_gain * real_cot + imag_gain * imag_cot).astype(BF16)
            modes[high, :] = (real_gain * imag_cot - imag_gain * real_cot).astype(BF16)
            first = real_cot * real_part + imag_cot * imag_part
            second = imag_cot * real_part - real_cot * imag_part
            fs[h, pl.ds(9 * n, 9)] = first.astype(BF16).reshape(9, 16, LANES)
            fs[h, pl.ds(48 + 9 * n, 9)] = second.astype(BF16).reshape(9, 16, LANES)
            return carry

        lax.fori_loop(0, WAVES // STEP, back, 0)
        to_field(3, zs, h)
        spread_start(zs, s2, h, 3)
        own_piece(zs, s2, h)
        lat_spread(lambda peer: fs.at[h, pl.ds(6 * peer, 6)], fr.at[h, lat], 1 + h)
        fr[h, lat] = fs[h, pl.ds(6 * lat, 6)]

    halo_wait(pslab, ptail, 8)
    apply_band(vb_ref, pslab)

    wait_bytes(wr.at[pl.ds(0, ROWS - 1)], ar_recv.at[0])
    w2s[...] = jnp.sum(wr[...].astype(F32), axis=0).astype(BF16)
    for h in range(2):
        wait_bytes(fr.at[h, pl.ds(0, ROWS - 1)], ar_recv.at[1 + h])
        f2s[6 * h : 6 * (h + 1)] = jnp.sum(fr[h].astype(F32), axis=0).astype(BF16)

    def to_owner(source, target, owner, index):
        @pl.when(me != owner)
        def _():
            pltpu.make_async_remote_copy(
                src_ref=source,
                dst_ref=target.at[me],
                send_sem=ar_send.at[index],
                recv_sem=ar_recv.at[index],
                device_id={"lon": owner},
                device_id_type=MESH,
            ).start()

    for o in range(12):
        to_owner(f2s.at[o], f2r, o, 3)
    for o in range(3):
        to_owner(w2s.at[o], w2r, 12 + o, 4)

    mix(True)

    def own_sum(source, work, target, slot, index, out_index):
        wait_bytes(work.at[pl.ds(0, ROWS - 1)], ar_recv.at[index])
        work[me] = source[slot]
        target[slot] = jnp.sum(work[...].astype(F32), axis=0).astype(BF16)

        def body(step, carry):
            peer = lax.rem(me + step, ROWS)
            pltpu.make_async_remote_copy(
                src_ref=target.at[slot],
                dst_ref=target.at[slot],
                send_sem=ar_send.at[out_index],
                recv_sem=ar_recv.at[out_index],
                device_id={"lon": peer},
                device_id_type=MESH,
            ).start()
            return carry

        lax.fori_loop(1, ROWS, body, 0)

    is_f = me < 12
    is_w = (me >= 12) & (me < 15)

    @pl.when(is_f)
    def _():
        own_sum(f2s, f2r, f3, me, 3, 5)

    @pl.when(is_w)
    def _():
        own_sum(w2s, w2r, w3, me - 12, 4, 6)

    def finish(h):
        lanes = slice(h * LANES, (h + 1) * LANES)
        spread_wait(s2, h, 3)

        def body(i, carry):
            value = dense[i, :, lanes] + s2[h, i].astype(F32)
            gin_ref[i, :, lanes] = (cts[i, :, lanes].astype(F32) + value).astype(BF16)
            return carry

        lax.fori_loop(0, ROWS, body, 0)

    finish(0)

    @pl.when(is_f)
    def _():
        wait_bytes(f3.at[pl.ds(0, 11)], ar_recv.at[5])

    @pl.when(jnp.logical_not(is_f))
    def _():
        wait_bytes(f3, ar_recv.at[5])

    @pl.when(is_w)
    def _():
        wait_bytes(w3.at[pl.ds(0, 2)], ar_recv.at[6])

    @pl.when(jnp.logical_not(is_w))
    def _():
        wait_bytes(w3, ar_recv.at[6])

    lat_spread(lambda peer: f3, ffin.at[lat], 7)
    lat_spread(lambda peer: w3, wfin.at[lat], 8)
    ffin[lat] = f3[...]
    wfin[lat] = w3[...]

    finish(1)

    wait_bytes(wfin.at[pl.ds(0, ROWS - 1)], ar_recv.at[8])
    gw_ref[...] = wfin[...].reshape(3 * CHANNELS, CHANNELS)
    wait_bytes(ffin.at[pl.ds(0, ROWS - 1)], ar_recv.at[7])

    def unpack(s, carry):
        rows = pl.ds(pl.multiple_of(s * PAD, PAD), PAD)
        for h in range(2):
            gf_ref[rows, h * LANES : (h + 1) * LANES] = ffin[s, 6 * h : 6 * (h + 1)].reshape(
                PAD, LANES
            )
        return carry

    lax.fori_loop(0, ROWS, unpack, 0)

    for phase, source in enumerate((xs, ys, ps, zs)):
        for h in range(2):
            wait_bytes(source.at[h, pl.ds(0, ROWS - 1)], a_send.at[phase, h])
    halo_end(slab, tail, 0)
    halo_end(pslab, ptail, 8)
    wait_bytes(wr.at[pl.ds(0, ROWS - 1)], ar_send.at[0])
    for h in range(2):
        wait_bytes(fr.at[h, pl.ds(0, ROWS - 1)], ar_send.at[1 + h])

    @pl.when(is_f)
    def _():
        wait_bytes(f2s.at[pl.ds(0, 11)], ar_send.at[3])
        wait_bytes(f2r.at[pl.ds(0, ROWS - 1)], ar_send.at[5])

    @pl.when(jnp.logical_not(is_f))
    def _():
        wait_bytes(f2s, ar_send.at[3])

    @pl.when(is_w)
    def _():
        wait_bytes(w2s.at[pl.ds(0, 2)], ar_send.at[4])
        wait_bytes(w2r.at[pl.ds(0, ROWS - 1)], ar_send.at[6])

    @pl.when(jnp.logical_not(is_w))
    def _():
        wait_bytes(w2s, ar_send.at[4])

    wait_bytes(ffin.at[pl.ds(0, ROWS - 1)], ar_send.at[7])
    wait_bytes(wfin.at[pl.ds(0, ROWS - 1)], ar_send.at[8])


def circular(vectors):
    ahead, behind = vectors[..., SPREAD:], vectors[..., :SPREAD]
    gap = jnp.zeros(vectors.shape[:-1] + (WIDE - 2 * SPREAD - 1,), vectors.dtype)
    return jnp.concatenate([ahead, gap, behind], axis=-1)


def on_device(features, cotangent, disco_basis, support_width, mix_weight, spectral_filter):
    effective = masked_basis(disco_basis, support_width).astype(F32)
    padded_basis = jnp.pad(effective, ((0, 0), (1, 1), (0, 0), (0, 0)))
    local = lax.dynamic_slice_in_dim(padded_basis, lax.axis_index("lat") * ROWS, ROWS + 2, 1)
    ahead = jnp.transpose(local[:, 1 : ROWS + 1], (1, 0, 2, 3))
    behind = jnp.stack([local[:, r : r + ROWS, 2 - r, ::-1] for r in range(3)], axis=2)
    behind = jnp.transpose(behind, (1, 0, 2, 3))
    ahead = circular(ahead).reshape(ROWS, 9, WIDE)
    behind = circular(behind).reshape(ROWS, 9, WIDE)
    tables = [jnp.asarray(t) for t in dft_tables()]

    vmem = pl.BlockSpec(memory_space=pltpu.VMEM)
    hbm = pl.BlockSpec(memory_space=pl.ANY)
    pieces = (2, ROWS, PAD, LANES)
    out, gin, gw, gf = pl.pallas_call(
        kernel,
        out_shape=[
            jax.ShapeDtypeStruct((ROWS, PAD, CHANNELS), BF16),
            jax.ShapeDtypeStruct((ROWS, PAD, CHANNELS), BF16),
            jax.ShapeDtypeStruct((3 * CHANNELS, CHANNELS), BF16),
            jax.ShapeDtypeStruct((2 * WAVES_PAD, CHANNELS), BF16),
        ],
        in_specs=[vmem] * 6 + [hbm] * 4,
        out_specs=[vmem] * 4,
        scratch_shapes=[
            pltpu.VMEM((4, ROWS * PAD, ROWS * PAD), BF16),
            pltpu.VMEM((ROWS, PAD, CHANNELS), BF16),
            pltpu.VMEM((ROWS + 2, WIDE, CHANNELS), BF16),
            pltpu.VMEM((ROWS + 2, WIDE, CHANNELS), BF16),
            pltpu.VMEM((ROWS + 2, SPREAD, CHANNELS), BF16),
            pltpu.VMEM((ROWS + 2, SPREAD, CHANNELS), BF16),
        ]
        + [pltpu.VMEM(pieces, BF16)] * 8
        + [
            pltpu.VMEM((3, ROWS, PAD, CHANNELS), BF16),
            pltpu.VMEM((ROWS, PAD, CHANNELS), F32),
            pltpu.VMEM((2, 2 * WAVES_PAD, LANES), F32),
            pltpu.VMEM((2 * WAVES_PAD, LANES), F32),
            pltpu.VMEM((2 * WAVES_PAD, LANES), BF16),
            pltpu.VMEM((3 * PAD, 3 * WIDE), BF16),
            pltpu.VMEM((48, 16, CHANNELS), BF16),
            pltpu.VMEM((ROWS, 3, 16, CHANNELS), BF16),
            pltpu.VMEM((3, 16, CHANNELS), BF16),
            pltpu.VMEM((ROWS, 16, CHANNELS), BF16),
            pltpu.VMEM((3, 16, CHANNELS), BF16),
            pltpu.VMEM((ROWS, 3, 16, CHANNELS), BF16),
            pltpu.VMEM((2, 96, 16, LANES), BF16),
            pltpu.VMEM((2, ROWS, 6, 16, LANES), BF16),
            pltpu.VMEM((12, 16, LANES), BF16),
            pltpu.VMEM((ROWS, 16, LANES), BF16),
            pltpu.VMEM((12, 16, LANES), BF16),
            pltpu.VMEM((ROWS, 12, 16, LANES), BF16),
            pltpu.SemaphoreType.DMA((4,)),
            pltpu.SemaphoreType.DMA((4, 2)),
            pltpu.SemaphoreType.DMA((4, 2)),
            pltpu.SemaphoreType.DMA((16,)),
            pltpu.SemaphoreType.DMA((16,)),
            pltpu.SemaphoreType.DMA((9,)),
            pltpu.SemaphoreType.DMA((9,)),
        ],
        compiler_params=pltpu.CompilerParams(
            collective_id=0, has_side_effects=True, vmem_limit_bytes=60 * 1024 * 1024
        ),
        cost_estimate=pl.CostEstimate(
            flops=8_000_000_000, bytes_accessed=30_000_000, transcendentals=400_000
        ),
    )(features, cotangent, ahead, behind, mix_weight, spectral_filter, *tables)
    return (
        out[:, :COLS],
        gin[:, :COLS],
        gw.astype(F32).reshape(3, CHANNELS, CHANNELS),
        gf.reshape(2, WAVES_PAD, CHANNELS)[:, :WAVES].astype(F32),
    )


def solution(mesh):
    return jax.shard_map(
        on_device,
        mesh=mesh,
        in_specs=(P("lat", "lon", None), P("lat", "lon", None), P(), P(), P(), P()),
        out_specs=(P("lat", "lon", None), P("lat", "lon", None), P(), P()),
        check_vma=False,
    )
```

time: 467 us -> 140 us (0.30)
  the two profiles are of different devices: /device:TPU:2 before, /device:TPU:1 now
where the time goes in v2:
time: 140 us
  Pallas kernels  124 us (89%)
  local copies, waits for them, and re-layouts  10.2 us (7%)
  other arithmetic  4.28 us (3%)
    pallas_call x1, Pallas kernels, on_device(): pl.pallas_call(kernel, out_shape=[jax.ShapeDtypeStruct((ROWS, PAD, CHANNE...  124 us
    unnamed x11, local copies, waits for them, and re-layouts  8.39 us

profile of v2, /device:TPU:1, one launch (start us, length us, event | category | flops | bytes accessed | tf_op | source)
XLA Modules:
  0.0 139.6 jit_solution(14886979887070808362)
XLA Ops:
  0.6 0.0 copy-start.1
  0.6 0.0 copy-start
  0.7 0.1 pad.16.clone
  0.7 0.9 broadcast_compare_fusion
  1.7 1.3 copy.22
  3.0 0.1 rev.9
  3.1 0.1 rev.10
  3.2 0.1 rev.11
  3.3 0.1 slice.50
  3.4 0.1 slice.45
  3.5 0.1 pad_maximum_fusion.1
  3.6 0.7 copy.25.vf_ref
  4.3 0.7 copy.26.vb_ref
  4.9 0.0 copy-done
  4.9 1.1 copy.23.x_ref
  6.1 0.0 copy-done.1
  6.1 1.1 copy.24.ct_ref
  7.2 124.4 %shard_map.129 = (bf16[16,96,256]{2,1,0:T(8,128)(2,1)}, bf16[16,96,256]{2,1,0:T(8,128)(2,1)}, bf16[768,256]{1,0:T(8,128)(2,1)}, bf16[1536,256]{1,0:T(8,128)(2,1)}) custom-call(bf16[16,90,256]{2,1,0:T(8,128)(2,1)} %copy.23.x_ref, bf16[16,90,256]{2,1,0:T(8,128)(2,1)} %copy.24.ct_ref, f32[16,9,128]{2,1,0:T(8,128)} %copy.25.vf_ref, f32[16,9,128]{2,1,0:T(8,128)} %copy.26.vb_ref, ...), custom_call_target="tpu_custom_call" | custom-call | flops 8000000000 | bytes 30000000 | tf_op jit(solution)/shard_map/pallas_call | solution.py:576
  131.6 0.0 copy-start.2
  131.6 2.5 %copy.27 = bf16[16,90,256]{2,0,1:T(8,128)(2,1)} copy(bf16[16,90,256]{2,1,0:T(8,128)(2,1)} %bitcast.14) | data formatting | bytes 1474560
  134.1 2.4 %copy.28 = bf16[16,90,256]{2,0,1:T(8,128)(2,1)} copy(bf16[16,90,256]{2,1,0:T(8,128)(2,1)} %bitcast.13) | data formatting | bytes 1474560
  136.5 1.9 %convert.3 = f32[3,256,256]{2,1,0:T(8,128)} convert(bf16[3,256,256]{2,1,0:T(8,128)(2,1)} %bitcast.18) | non-fusion elementwise | flops 196608 | bytes 1179648 | tf_op jit(solution)/shard_map/reshape | solution.py:632
  138.4 0.0 copy-done.2
  138.4 1.2 slice_convert_fusion
  (7 shorter events, 0.1 us)
Async XLA Ops:
  0.6 5.4 %copy-start.1 = (bf16[16,90,256]{2,0,1:T(8,128)(2,1)S(1)}, bf16[16,90,256]{2,0,1:T(8,128)(2,1)}, u32[]{:S(2)}) copy-start(bf16[16,90,256]{2,0,1:T(8,128)(2,1)} %param.11) | copy-start | bytes 2211844
  0.6 4.3 %copy-start = (bf16[16,90,256]{2,0,1:T(8,128)(2,1)S(1)}, bf16[16,90,256]{2,0,1:T(8,128)(2,1)}, u32[]{:S(2)}) copy-start(bf16[16,90,256]{2,0,1:T(8,128)(2,1)} %param.10) | copy-start | bytes 2211844
  131.6 6.8 %copy-start.2 = (bf16[1536,256]{1,0:T(8,128)(2,1)S(1)}, bf16[1536,256]{1,0:T(8,128)(2,1)}, u32[]{:S(2)}) copy-start(bf16[1536,256]{1,0:T(8,128)(2,1)} %get-tuple-element.11) | copy-start | bytes 2359300

commit v3 on v2

v3 whole, which is shorter than its diff:
```python
import math

import jax
import jax.numpy as jnp
import ml_dtypes
import numpy as np
from jax import lax
from jax.experimental import pallas as pl
from jax.experimental.pallas import tpu as pltpu
from jax.sharding import PartitionSpec as P

MESH = pl.DeviceIdType.MESH
F32 = jnp.float32
BF16 = jnp.bfloat16

ROWS = 16
COLS = 90
PAD = 96
WAVES = 720
WAVES_PAD = 768
SPREAD = 16
LANES = 128
CHANNELS = 256
WIDE = 128
TILE = 384


def dft_tables():
    longitudes = ROWS * COLS
    cell_index = np.arange(longitudes, dtype=np.int64)
    wave_index = np.arange(WAVES, dtype=np.int64)
    phase_index = wave_index[:, None] * cell_index[None, :] % longitudes
    angles = phase_index.astype(np.float32) * np.float32(2.0 * math.pi / longitudes)
    cosine_wave = np.cos(angles)
    sine_wave = np.sin(angles)
    factor = np.where(wave_index == 0, 1.0, 2.0).astype(np.float32) / np.float32(longitudes)

    def padded(real, imag):
        table = np.zeros((2, WAVES_PAD, ROWS, PAD), np.float32)
        table[0, :WAVES, :, :COLS] = real.reshape(WAVES, ROWS, COLS)
        table[1, :WAVES, :, :COLS] = imag.reshape(WAVES, ROWS, COLS)
        return table.reshape(2 * WAVES_PAD, ROWS * PAD).astype(ml_dtypes.bfloat16)

    forward = padded(cosine_wave, -sine_wave)
    inverse_t = padded(cosine_wave * factor[:, None], -sine_wave * factor[:, None])
    return (
        forward,
        np.ascontiguousarray(inverse_t.T),
        inverse_t,
        np.ascontiguousarray(forward.T),
    )


def kernel(
    x_ref, ct_ref, basis_ref, width_ref, mix_ref, sf_ref, t0_ref, t1_ref, t2_ref, t3_ref,
    out_ref, gin_ref, gw_ref, gf_ref,
    tables, ctv, mixv, sfv, perm, vf, vb, cts, slab, pslab, tail, ptail,
    xs, g1, ys, s1, ps, g2, zs, s2,
    resp, dense, spectrum, cotspec, modes, band, outs, folded, gfold,
    parts, pair_in, pair_sum, lat_in, lat_sum, z_in, total,
    load_sem, store_sem, a_send, a_recv, halo_send, halo_recv, ar_send, ar_recv,
):
    me = lax.axis_index("lon")
    lat = lax.axis_index("lat")
    right = lax.rem(me + 1, ROWS)
    left = lax.rem(me + ROWS - 1, ROWS)
    core = lax.rem(me, 2)
    chip = lax.div(me, 2)
    twin = me + 1 - 2 * core

    loads = [
        pltpu.make_async_copy(ref, target, load_sem.at[i])
        for i, (ref, target) in enumerate(
            (
                (ct_ref, ctv),
                (t0_ref, tables.at[0]),
                (sf_ref, sfv),
                (t1_ref, tables.at[1]),
                (mix_ref, mixv),
                (t2_ref, tables.at[2]),
                (t3_ref, tables.at[3]),
            )
        )
    ]
    for copy in loads:
        copy.start()

    barrier = pltpu.get_barrier_semaphore()

    def greet(step, carry):
        pl.semaphore_signal(
            barrier, inc=1, device_id={"lon": lax.rem(me + step, ROWS)}, device_id_type=MESH
        )
        pl.semaphore_signal(
            barrier, inc=1, device_id={"lat": lax.rem(lat + step, ROWS)}, device_id_type=MESH
        )
        return carry

    lax.fori_loop(1, ROWS, greet, 0)

    a = lax.broadcasted_iota(jnp.int32, (256, 256), 0)
    b = lax.broadcasted_iota(jnp.int32, (256, 256), 1)
    perm[...] = jnp.where(b == (a & 15) * 16 + (a >> 4), 1.0, 0.0).astype(BF16)

    def unfold(source, store):
        for g in range(6):
            count = min(16, COLS - 16 * g)
            data = source[16 * g : 16 * g + count].reshape(count * ROWS, CHANNELS)
            value = jnp.dot(perm[:, 0 : count * ROWS], data, preferred_element_type=F32)
            store(slice(16 * g, 16 * g + 16), value.astype(BF16).reshape(ROWS, 16, CHANNELS))

    def fold(source, target, lanes):
        for g in range(6):
            count = min(16, COLS - 16 * g)
            data = source[:, 16 * g : 16 * g + 16, lanes]
            width = data.shape[2]
            value = jnp.dot(perm[...], data.reshape(256, width), preferred_element_type=F32)
            value = value.astype(BF16).reshape(16, ROWS, width)
            target[16 * g : 16 * g + count, :, lanes] = value[0:count]

    def store_x(columns, value):
        slab[1:17, columns, :] = value
        for h in range(2):
            xs[h, :, columns, :] = value[:, :, h * LANES : (h + 1) * LANES]

    def store_ct(columns, value):
        cts[:, columns, :] = value

    unfold(x_ref, store_x)
    pl.semaphore_wait(barrier, 2 * (ROWS - 1))

    def offset(step):
        return 8 + (1 - 2 * lax.rem(step, 2)) * lax.div(step + 1, 2)

    def spread_start(source, target, h, phase, first=0, end=ROWS - 1):
        def body(step, carry):
            peer = lax.rem(me + offset(step), ROWS)
            pltpu.make_async_remote_copy(
                src_ref=source.at[h, peer],
                dst_ref=target.at[h, me],
                send_sem=a_send.at[phase, h],
                recv_sem=a_recv.at[phase, h],
                device_id={"lon": peer},
                device_id_type=MESH,
            ).start()
            return carry

        lax.fori_loop(first, end, body, 0)

    def own_piece(source, target, h):
        target[h, me] = source[h, me]

    def wait_bytes(ref, sem):
        pltpu.make_async_copy(ref, ref, sem).wait()

    def spread_wait(target, h, phase):
        wait_bytes(target.at[h, pl.ds(0, ROWS - 1)], a_recv.at[phase, h])

    def halo_copy(src, dst, index, device):
        return pltpu.make_async_remote_copy(
            src_ref=src,
            dst_ref=dst,
            send_sem=halo_send.at[index],
            recv_sem=halo_recv.at[index],
            device_id=device,
            device_id_type=MESH,
        )

    def lat_halo(buf, base):
        up = halo_copy(
            buf.at[1, pl.ds(0, PAD)], buf.at[17, pl.ds(0, PAD)], base, {"lat": lax.max(lat - 1, 0)}
        )
        down = halo_copy(
            buf.at[16, pl.ds(0, PAD)],
            buf.at[0, pl.ds(0, PAD)],
            base + 1,
            {"lat": lax.min(lat + 1, ROWS - 1)},
        )
        return up, down

    def lon_halo(buf, end, base):
        pairs = []
        for n, rows in enumerate((pl.ds(1, ROWS), pl.ds(0, 1), pl.ds(17, 1))):
            pairs.append(
                (
                    halo_copy(
                        buf.at[rows, pl.ds(0, SPREAD)],
                        buf.at[rows, pl.ds(PAD, SPREAD)],
                        base + 2 + 2 * n,
                        {"lon": left},
                    ),
                    halo_copy(
                        end.at[rows],
                        buf.at[rows, pl.ds(PAD + SPREAD, SPREAD)],
                        base + 3 + 2 * n,
                        {"lon": right},
                    ),
                )
            )
        return pairs

    def tail_row(buf, end, i):
        moved = pltpu.roll(buf[i, 0:PAD, :].astype(F32), PAD - COLS, 0)
        end[i] = moved[PAD - SPREAD : PAD].astype(BF16)

    def halo_begin(buf, end, base):
        up, down = lat_halo(buf, base)

        @pl.when(lat > 0)
        def _():
            up.start()

        @pl.when(lat < ROWS - 1)
        def _():
            down.start()

        def body(i, carry):
            tail_row(buf, end, i + 1)
            return carry

        lax.fori_loop(0, ROWS, body, 0)
        for copy in lon_halo(buf, end, base)[0]:
            copy.start()

    def halo_middle(buf, end, base):
        up, down = lat_halo(buf, base)

        @pl.when(lat > 0)
        def _():
            down.wait_recv()

        @pl.when(lat == 0)
        def _():
            buf[0, 0:PAD, :] = jnp.zeros((PAD, CHANNELS), BF16)

        @pl.when(lat < ROWS - 1)
        def _():
            up.wait_recv()

        @pl.when(lat == ROWS - 1)
        def _():
            buf[17, 0:PAD, :] = jnp.zeros((PAD, CHANNELS), BF16)

        tail_row(buf, end, 0)
        tail_row(buf, end, 17)
        for pair in lon_halo(buf, end, base)[1:]:
            for copy in pair:
                copy.start()

    def halo_wait_main(buf, end, base):
        for copy in lon_halo(buf, end, base)[0]:
            copy.wait_recv()

    def halo_wait_edge(buf, end, base):
        for pair in lon_halo(buf, end, base)[1:]:
            for copy in pair:
                copy.wait_recv()

    def halo_end(buf, end, base):
        up, down = lat_halo(buf, base)

        @pl.when(lat > 0)
        def _():
            up.wait_send()

        @pl.when(lat < ROWS - 1)
        def _():
            down.wait_send()

        for pair in lon_halo(buf, end, base):
            for copy in pair:
                copy.wait_send()

    lane = lax.broadcasted_iota(jnp.int32, (PAD, WIDE), 1)
    row = lax.broadcasted_iota(jnp.int32, (PAD, WIDE), 0)
    direct = (row < COLS) & ((lane < COLS) | (lane >= PAD + SPREAD))
    shifted = (row < COLS) & (lane >= PAD) & (lane < PAD + SPREAD)

    def band_row(vecs, buf, i, backward):
        for k in range(3):
            for r in range(3):
                if backward:
                    vec = vecs[3 * k + 2 - r, pl.ds(i + r, 1), :]
                else:
                    vec = vecs[3 * k + r, pl.ds(i + 1, 1), :]
                near = pltpu.roll(jnp.broadcast_to(vec, (PAD, WIDE)), 0, 1, stride=1, stride_axis=0)
                far = pltpu.roll(
                    jnp.broadcast_to(vec, (32, WIDE)), 64 + PAD - COLS, 1, stride=1, stride_axis=0
                )
                high = jnp.where(direct[64:], near[64:], jnp.where(shifted[64:], far, 0.0))
                lanes = slice(r * WIDE, (r + 1) * WIDE)
                band[k * PAD : k * PAD + 64, lanes] = jnp.where(direct[:64], near[:64], 0.0).astype(
                    BF16
                )
                band[k * PAD + 64 : (k + 1) * PAD, lanes] = high.astype(BF16)
        around = buf[pl.ds(i, 3)].reshape(3 * WIDE, CHANNELS)
        value = jnp.dot(band[...], around, preferred_element_type=F32).astype(BF16)
        for k in range(3):
            resp[k, i] = value[k * PAD : (k + 1) * PAD]

    def inner_rows(vecs, buf, backward):
        def body(i, carry):
            band_row(vecs, buf, i, backward)
            return carry

        lax.fori_loop(1, ROWS - 1, body, 0)

    def edge_rows(vecs, buf, backward):
        def body(n, carry):
            band_row(vecs, buf, n * (ROWS - 1), backward)
            return carry

        lax.fori_loop(0, 2, body, 0)

    def tap_vectors():
        offsets = jnp.abs(lax.broadcasted_iota(jnp.int32, (33, 256), 0) - SPREAD)
        retained = offsets <= width_ref[...]
        first = lax.broadcasted_iota(jnp.int32, (32, 256), 0) + lat * ROWS - 1
        chosen = jnp.where(lax.broadcasted_iota(jnp.int32, (32, 256), 1) == first, 1.0, 0.0)
        tap = lax.broadcasted_iota(jnp.int32, (33, WIDE), 0)
        spot = lax.broadcasted_iota(jnp.int32, (33, WIDE), 1)
        ahead = jnp.where(((tap + WIDE - SPREAD) & (WIDE - 1)) == spot, 1.0, 0.0).astype(BF16)
        behind = jnp.where(((WIDE + SPREAD - tap) & (WIDE - 1)) == spot, 1.0, 0.0).astype(BF16)
        for k in range(3):
            for r in range(3):
                kept = jnp.where(retained, basis_ref[k, r].astype(F32), 0.0).astype(BF16)
                local = lax.dot_general(
                    chosen.astype(BF16), kept, (((1,), (1,)), ((), ())), preferred_element_type=F32
                ).astype(BF16)
                vf[3 * k + r] = jnp.dot(local, ahead, preferred_element_type=F32)
                vb[3 * k + r] = jnp.dot(local, behind, preferred_element_type=F32)

    def mix(transposed):
        def body(n, carry):
            total = jnp.zeros((TILE, CHANNELS), F32)
            for k in range(3):
                part = resp[k, pl.ds(4 * n, 4)].reshape(TILE, CHANNELS)
                total = total + lax.dot_general(
                    part,
                    mixv[k],
                    (((1,), (1 if transposed else 0,)), ((), ())),
                    preferred_element_type=F32,
                )
            dense[pl.ds(4 * n, 4)] = total.reshape(4, PAD, CHANNELS)
            return carry

        lax.fori_loop(0, 4, body, 0)

    def to_spectrum(table, field, h, target):
        def body(n, carry):
            rows = pl.ds(pl.multiple_of(n * TILE, TILE), TILE)
            target[rows, :] = jnp.dot(
                tables[table, rows, :],
                field[h].reshape(ROWS * PAD, LANES),
                preferred_element_type=F32,
            )
            return carry

        lax.fori_loop(0, 4, body, 0)

    def to_field(table, field, h):
        def body(n, carry):
            rows = pl.ds(pl.multiple_of(n * TILE, TILE), TILE)
            value = jnp.dot(tables[table, rows, :], modes[...], preferred_element_type=F32)
            field[h, pl.ds(4 * n, 4)] = value.astype(BF16).reshape(4, PAD, LANES)
            return carry

        lax.fori_loop(0, 4, body, 0)

    def chunk_start(source, target, stage, q, device):
        pltpu.make_async_remote_copy(
            src_ref=source,
            dst_ref=target,
            send_sem=ar_send.at[stage, q],
            recv_sem=ar_recv.at[stage, q],
            device_id=device,
            device_id_type=MESH,
        ).start()

    def pair_start(q):
        chunk_start(parts.at[q, 1 - core], pair_in.at[q], 0, q, {"lon": twin})

    def to_lat(source, target, stage, q):
        def body(step, carry):
            peer = lax.rem(lat + step, ROWS)
            chunk_start(source(peer), target, stage, q, {"lat": peer})
            return carry

        lax.fori_loop(1, ROWS, body, 0)

    def pair_finish(q):
        wait_bytes(pair_in.at[q], ar_recv.at[0, q])

        def body(n, carry):
            rows = pl.ds(6 * n, 6)
            both = parts[q, core, rows].astype(F32) + pair_in[q, rows].astype(F32)
            pair_sum[q, rows] = both.astype(BF16)
            return carry

        lax.fori_loop(0, 8, body, 0)
        to_lat(lambda peer: pair_sum.at[q, pl.ds(3 * peer, 3)], lat_in.at[q, lat], 1, q)
        lat_in[q, lat] = pair_sum[q, pl.ds(3 * lat, 3)]

    def lat_finish(q):
        wait_bytes(lat_in.at[q, pl.ds(0, ROWS - 1)], ar_recv.at[1, q])
        value = jnp.sum(lat_in[q].astype(F32), axis=0).astype(BF16)
        lat_sum[q] = value
        z_in[q, chip] = value

        def body(step, carry):
            peer = lax.rem(me + 2 * step, ROWS)
            chunk_start(lat_sum.at[q], z_in.at[q, chip], 2, q, {"lon": peer})
            return carry

        lax.fori_loop(1, ROWS // 2, body, 0)

    def z_finish(q):
        wait_bytes(z_in.at[q, pl.ds(0, ROWS // 2 - 1)], ar_recv.at[2, q])
        mine = pl.ds(3 * lat, 3)
        total[q, core, mine] = jnp.sum(z_in[q].astype(F32), axis=0).astype(BF16)
        to_lat(lambda peer: total.at[q, core, mine], total.at[q, core, mine], 3, q)

    def gather_finish(q):
        wait_bytes(total.at[q, 0, pl.ds(0, 45)], ar_recv.at[3, q])
        chunk_start(total.at[q, core], total.at[q, core], 4, q, {"lon": twin})

    def chunk_wait(q):
        wait_bytes(total.at[q, 0], ar_recv.at[4, q])

    def chunk_end(q):
        wait_bytes(total.at[q, 0], ar_send.at[0, q])
        wait_bytes(total.at[q, 0, pl.ds(0, 45)], ar_send.at[1, q])
        wait_bytes(total.at[q, 0, pl.ds(0, 21)], ar_send.at[2, q])
        wait_bytes(total.at[q, 0, pl.ds(0, 45)], ar_send.at[3, q])
        wait_bytes(total.at[q, 0], ar_send.at[4, q])

    spread_start(xs, g1, 0, 0)
    halo_begin(slab, tail, 0)
    spread_start(xs, g1, 1, 0)
    for h in range(2):
        own_piece(xs, g1, h)
    tap_vectors()
    loads[0].wait()
    unfold(ctv, store_ct)
    modes[WAVES:WAVES_PAD, :] = jnp.zeros((WAVES_PAD - WAVES, LANES), BF16)
    modes[WAVES_PAD + WAVES :, :] = jnp.zeros((WAVES_PAD - WAVES, LANES), BF16)
    for h in range(2):
        for c in range(2):
            parts[1 + h, c, 45:48] = jnp.zeros((3, 16, LANES), BF16)
    halo_middle(slab, tail, 0)
    STEP = 144
    for copy in loads[1:]:
        copy.wait()

    for h in range(2):
        lanes = slice(h * LANES, (h + 1) * LANES)
        spread_wait(g1, h, 0)
        to_spectrum(0, g1, h, spectrum.at[h])

        def gain(n, carry):
            low = pl.ds(pl.multiple_of(n * STEP, 16), STEP)
            high = pl.ds(pl.multiple_of(WAVES_PAD + n * STEP, 16), STEP)
            real_part, imag_part = spectrum[h, low, :], spectrum[h, high, :]
            real_gain, imag_gain = sfv[0, low, lanes], sfv[1, low, lanes]
            modes[low, :] = (real_gain * real_part - imag_gain * imag_part).astype(BF16)
            modes[high, :] = (real_gain * imag_part + imag_gain * real_part).astype(BF16)
            return carry

        lax.fori_loop(0, WAVES // STEP, gain, 0)
        to_field(1, ys, h)
        spread_start(ys, s1, h, 1)
        own_piece(ys, s1, h)
        if h == 0:
            halo_wait_main(slab, tail, 0)
            inner_rows(vf, slab, False)

    halo_wait_edge(slab, tail, 0)
    edge_rows(vf, slab, False)
    mix(False)

    for h in range(2):
        lanes = slice(h * LANES, (h + 1) * LANES)
        spread_wait(s1, h, 1)

        def activate(i, carry):
            preact = dense[i, :, lanes] + s1[h, i].astype(F32)
            logistic = 1.0 / (1.0 + jnp.exp(-preact))
            own = slab[i + 1, 0:PAD, lanes].astype(F32)
            outs[i, :, lanes] = (own + preact * logistic).astype(BF16)
            slope = logistic * (1.0 + preact * (1.0 - logistic))
            grad = (cts[i, :, lanes].astype(F32) * slope).astype(BF16)
            ps[h, i] = grad
            pslab[i + 1, 0:PAD, lanes] = grad
            return carry

        lax.fori_loop(0, ROWS, activate, 0)
        if h == 1:
            halo_begin(pslab, ptail, 8)
        spread_start(ps, g2, h, 2)
        own_piece(ps, g2, h)

    for k in range(3):
        part = lax.dot_general(
            resp[k].reshape(ROWS * PAD, CHANNELS),
            pslab[1:17, 0:PAD, :].reshape(ROWS * PAD, CHANNELS),
            (((0,), (0,)), ((), ())),
            preferred_element_type=F32,
        ).astype(BF16)
        for c in range(2):
            parts[0, c, 16 * k : 16 * (k + 1)] = part[:, c * LANES : (c + 1) * LANES].reshape(
                16, 16, LANES
            )
    pair_start(0)
    halo_middle(pslab, ptail, 8)
    fold(outs, folded, slice(0, CHANNELS))
    out_store = pltpu.make_async_copy(folded, out_ref, store_sem.at[0])
    out_store.start()

    for h in range(2):
        lanes = slice(h * LANES, (h + 1) * LANES)
        spread_wait(g2, h, 2)
        to_spectrum(2, g2, h, cotspec)

        def back(n, carry):
            low = pl.ds(pl.multiple_of(n * STEP, 16), STEP)
            high = pl.ds(pl.multiple_of(WAVES_PAD + n * STEP, 16), STEP)
            real_part, imag_part = spectrum[h, low, :], spectrum[h, high, :]
            real_cot, imag_cot = cotspec[low, :], cotspec[high, :]
            real_gain, imag_gain = sfv[0, low, lanes], sfv[1, low, lanes]
            modes[low, :] = (real_gain * real_cot + imag_gain * imag_cot).astype(BF16)
            modes[high, :] = (real_gain * imag_cot - imag_gain * real_cot).astype(BF16)
            first = real_cot * real_part + imag_cot * imag_part
            second = imag_cot * real_part - real_cot * imag_part
            parts[1 + h, 0, pl.ds(9 * n, 9)] = first.astype(BF16).reshape(9, 16, LANES)
            parts[1 + h, 1, pl.ds(9 * n, 9)] = second.astype(BF16).reshape(9, 16, LANES)
            return carry

        lax.fori_loop(0, WAVES // STEP, back, 0)
        pair_start(1 + h)
        if h == 0:
            pair_finish(0)
        to_field(3, zs, h)
        if h == 0:
            spread_start(zs, s2, h, 3)
            own_piece(zs, s2, h)
            pair_finish(1)
            halo_wait_main(pslab, ptail, 8)
            inner_rows(vb, pslab, True)
            lat_finish(0)
        else:
            pair_finish(2)
            spread_start(zs, s2, h, 3, 0, 8)
            own_piece(zs, s2, h)

    lat_finish(1)
    halo_wait_edge(pslab, ptail, 8)
    edge_rows(vb, pslab, True)
    lat_finish(2)
    spread_start(zs, s2, 1, 3, 8, ROWS - 1)
    mix(True)
    z_finish(0)

    def finish(h):
        lanes = slice(h * LANES, (h + 1) * LANES)
        spread_wait(s2, h, 3)

        def body(i, carry):
            value = dense[i, :, lanes] + s2[h, i].astype(F32)
            outs[i, :, lanes] = (cts[i, :, lanes].astype(F32) + value).astype(BF16)
            return carry

        lax.fori_loop(0, ROWS, body, 0)
        fold(outs, gfold, lanes)
        store = pltpu.make_async_copy(
            gfold.at[:, :, lanes], gin_ref.at[:, :, lanes], store_sem.at[1 + h]
        )
        store.start()
        return store

    z_finish(1)
    finals = [finish(0)]
    z_finish(2)
    gather_finish(0)
    gather_finish(1)
    chunk_wait(0)
    for k in range(3):
        for c in range(2):
            gw_ref[k, :, c * LANES : (c + 1) * LANES] = (
                total[0, c, 16 * k : 16 * (k + 1)].reshape(CHANNELS, LANES).astype(F32)
            )
    def filter_out(h):
        chunk_wait(1 + h)
        for c in range(2):
            gf_ref[c, :, h * LANES : (h + 1) * LANES] = (
                total[1 + h, c, 0:45].reshape(WAVES, LANES).astype(F32)
            )

    filter_out(0)
    gather_finish(2)
    finals.append(finish(1))
    filter_out(1)

    for phase, source in enumerate((xs, ys, ps, zs)):
        for h in range(2):
            wait_bytes(source.at[h, pl.ds(0, ROWS - 1)], a_send.at[phase, h])
    halo_end(slab, tail, 0)
    halo_end(pslab, ptail, 8)
    for q in range(3):
        chunk_end(q)
    out_store.wait()
    for store in finals:
        store.wait()


def deliver(*refs):
    sources, targets, held, arrived, left = refs[0:4], refs[4:8], refs[8:12], refs[12], refs[13]
    loads = [pltpu.make_async_copy(sources[i], held[i], arrived.at[i]) for i in range(4)]
    stores = [pltpu.make_async_copy(held[i], targets[i], left.at[i]) for i in range(4)]
    for copy in loads:
        copy.start()
    for i in range(4):
        loads[i].wait()
        stores[i].start()
    for copy in stores:
        copy.wait()


def on_device(features, cotangent, disco_basis, support_width, mix_weight, spectral_filter):
    tables = [jnp.asarray(t) for t in dft_tables()]
    vmem = pl.BlockSpec(memory_space=pltpu.VMEM)
    hbm = pl.BlockSpec(memory_space=pl.ANY)
    pieces = (2, ROWS, PAD, LANES)
    out, gin, gw, gf = pl.pallas_call(
        kernel,
        out_shape=[
            jax.ShapeDtypeStruct((COLS, ROWS, CHANNELS), BF16),
            jax.ShapeDtypeStruct((COLS, ROWS, CHANNELS), BF16),
            jax.ShapeDtypeStruct((3, CHANNELS, CHANNELS), F32),
            jax.ShapeDtypeStruct((2, WAVES, CHANNELS), F32),
        ],
        in_specs=[vmem, hbm, vmem, vmem] + [hbm] * 6,
        out_specs=[hbm, hbm, vmem, vmem],
        scratch_shapes=[
            pltpu.VMEM((4, ROWS * PAD, ROWS * PAD), BF16),
            pltpu.VMEM((COLS, ROWS, CHANNELS), BF16),
            pltpu.VMEM((3, CHANNELS, CHANNELS), BF16),
            pltpu.VMEM((2, WAVES, CHANNELS), F32),
            pltpu.VMEM((256, 256), BF16),
            pltpu.VMEM((9, 32, WIDE), F32),
            pltpu.VMEM((9, 32, WIDE), F32),
            pltpu.VMEM((ROWS, PAD, CHANNELS), BF16),
            pltpu.VMEM((ROWS + 2, WIDE, CHANNELS), BF16),
            pltpu.VMEM((ROWS + 2, WIDE, CHANNELS), BF16),
            pltpu.VMEM((ROWS + 2, SPREAD, CHANNELS), BF16),
            pltpu.VMEM((ROWS + 2, SPREAD, CHANNELS), BF16),
        ]
        + [pltpu.VMEM(pieces, BF16)] * 8
        + [
            pltpu.VMEM((3, ROWS, PAD, CHANNELS), BF16),
            pltpu.VMEM((ROWS, PAD, CHANNELS), F32),
            pltpu.VMEM((2, 2 * WAVES_PAD, LANES), F32),
            pltpu.VMEM((2 * WAVES_PAD, LANES), F32),
            pltpu.VMEM((2 * WAVES_PAD, LANES), BF16),
            pltpu.VMEM((3 * PAD, 3 * WIDE), BF16),
            pltpu.VMEM((ROWS, PAD, CHANNELS), BF16),
            pltpu.VMEM((COLS, ROWS, CHANNELS), BF16),
            pltpu.VMEM((COLS, ROWS, CHANNELS), BF16),
            pltpu.VMEM((3, 2, 48, 16, LANES), BF16),
            pltpu.VMEM((3, 48, 16, LANES), BF16),
            pltpu.VMEM((3, 48, 16, LANES), BF16),
            pltpu.VMEM((3, ROWS, 3, 16, LANES), BF16),
            pltpu.VMEM((3, 3, 16, LANES), BF16),
            pltpu.VMEM((3, ROWS // 2, 3, 16, LANES), BF16),
            pltpu.VMEM((3, 2, 48, 16, LANES), BF16),
            pltpu.SemaphoreType.DMA((7,)),
            pltpu.SemaphoreType.DMA((3,)),
            pltpu.SemaphoreType.DMA((4, 2)),
            pltpu.SemaphoreType.DMA((4, 2)),
            pltpu.SemaphoreType.DMA((16,)),
            pltpu.SemaphoreType.DMA((16,)),
            pltpu.SemaphoreType.DMA((5, 3)),
            pltpu.SemaphoreType.DMA((5, 3)),
        ],
        compiler_params=pltpu.CompilerParams(
            collective_id=0, has_side_effects=True, vmem_limit_bytes=60 * 1024 * 1024
        ),
        cost_estimate=pl.CostEstimate(
            flops=8_000_000_000, bytes_accessed=30_000_000, transcendentals=400_000
        ),
    )(
        jnp.transpose(features, (1, 0, 2)),
        jnp.transpose(cotangent, (1, 0, 2)),
        jnp.transpose(disco_basis, (0, 2, 3, 1)),
        support_width.reshape(1, -1),
        mix_weight,
        spectral_filter,
        *tables,
    )
    results = (out, gin, gw, gf)
    out, gin, gw, gf = pl.pallas_call(
        deliver,
        out_shape=[jax.ShapeDtypeStruct(r.shape, r.dtype) for r in results],
        in_specs=[hbm] * 4,
        out_specs=[hbm] * 4,
        scratch_shapes=[pltpu.VMEM(r.shape, r.dtype) for r in results]
        + [pltpu.SemaphoreType.DMA((4,)), pltpu.SemaphoreType.DMA((4,))],
    )(*results)
    return (jnp.transpose(out, (1, 0, 2)), jnp.transpose(gin, (1, 0, 2)), gw, gf)


def solution(mesh):
    return jax.shard_map(
        on_device,
        mesh=mesh,
        in_specs=(P("lat", "lon", None), P("lat", "lon", None), P(), P(), P(), P()),
        out_specs=(P("lat", "lon", None), P("lat", "lon", None), P(), P()),
        check_vma=False,
    )
```

time: 140 us -> 106 us (0.76)
  Pallas kernels: 124 us -> 106 us
  local copies, waits for them, and re-layouts: 10.2 us -> 0 us
  other arithmetic: 4.28 us -> 0 us
    pallas_call x1 -> x2, Pallas kernels: 124 us -> 106 us  [the longest x1 102 us: on_device(): pl.pallas_call(kernel, out_shape=[jax.ShapeDtypeStruct((COLS, ROWS, CHANN...]
    unnamed x11 -> x0, local copies, waits for them, and re-layouts: 8.39 us -> none
    reshape x1 -> x0, other arithmetic: 1.94 us -> none  [on_device(): gw.astype(F32).reshape(3, CHANNELS, CHANNELS)]
where the time goes in v3:
time: 106 us
  Pallas kernels  106 us (100%)
    pallas_call x1, Pallas kernels, on_device(): pl.pallas_call(kernel, out_shape=[jax.ShapeDtypeStruct((COLS, ROWS, CHANN...  102 us
    pallas_call x1, Pallas kernels, on_device(): pl.pallas_call(deliver, out_shape=[jax.ShapeDtypeStruct(r.shape, r.dtype)...  3.24 us

profile of v3, /device:TPU:1, one launch (start us, length us, event | category | flops | bytes accessed | tf_op | source)
XLA Modules:
  0.0 106.2 jit_solution(4824866965808017293)
XLA Ops:
  0.6 102.3 %shard_map.129 = (bf16[90,16,256]{2,1,0:T(8,128)(2,1)}, bf16[90,16,256]{2,1,0:T(8,128)(2,1)}, f32[3,256,256]{2,1,0:T(8,128)}, f32[2,720,256]{2,1,0:T(8,128)}) custom-call(bf16[90,16,256]{2,1,0:T(8,128)(2,1)} %bitcast.6, bf16[90,16,256]{2,1,0:T(8,128)(2,1)} %bitcast.7, bf16[3,3,33,256]{3,2,1,0:T(8,128)(2,1)} %bitcast.10, s32[1,256]{1,0:T(1,128)} %bitcast.11, ...), custom_call_target="tpu_custom_call" | custom-call | flops 8000000000 | bytes 30000000 | tf_op jit(solution)/shard_map/pallas_call | solution.py:633
  103.0 3.2 %shard_map.130 = (bf16[90,16,256]{2,1,0:T(8,128)(2,1)}, bf16[90,16,256]{2,1,0:T(8,128)(2,1)}, f32[3,256,256]{2,1,0:T(8,128)}, f32[2,720,256]{2,1,0:T(8,128)}) custom-call(bf16[90,16,256]{2,1,0:T(8,128)(2,1)} %get-tuple-element.12.refs_0_, bf16[90,16,256]{2,1,0:T(8,128)(2,1)} %get-tuple-element.13.refs_1_, f32[3,256,256]{2,1,0:T(8,128)} %get-tuple-element.14.refs_2_, ...), custom_call_target="tpu_custom_call" | custom-call | tf_op jit(solution)/shard_map/pallas_call | solution.py:700

commit v4 on v3

--- a/solution.py
+++ b/solution.py
@@ -23,6 +23,7 @@
 CHANNELS = 256
 WIDE = 128
 TILE = 384
+SCATTERED = (0,)
 
 
 def dft_tables():
@@ -53,11 +54,11 @@
 
 def kernel(
     x_ref, ct_ref, basis_ref, width_ref, mix_ref, sf_ref, t0_ref, t1_ref, t2_ref, t3_ref,
-    out_ref, gin_ref, gw_ref, gf_ref,
+    out_ref, gin_ref, sum_ref,
     tables, ctv, mixv, sfv, perm, vf, vb, cts, slab, pslab, tail, ptail,
     xs, g1, ys, s1, ps, g2, zs, s2,
     resp, dense, spectrum, cotspec, modes, band, outs, folded, gfold,
-    parts, pair_in, pair_sum, lat_in, lat_sum, z_in, total,
+    parts, pair_in, pair_sum, lat_in, lat_sum, z_in, z_tile, total,
     load_sem, store_sem, a_send, a_recv, halo_send, halo_recv, ar_send, ar_recv,
 ):
     me = lax.axis_index("lon")
@@ -405,6 +406,21 @@
         wait_bytes(lat_in.at[q, pl.ds(0, ROWS - 1)], ar_recv.at[1, q])
         value = jnp.sum(lat_in[q].astype(F32), axis=0).astype(BF16)
         lat_sum[q] = value
+        if q in SCATTERED:
+            for t in range(3):
+                owner = 3 * q + t
+
+                @pl.when(chip == owner)
+                def _():
+                    z_tile[q, chip] = value[t]
+
+                @pl.when(chip != owner)
+                def _():
+                    chunk_start(
+                        lat_sum.at[q, t], z_tile.at[q, chip], 2, q, {"lon": 2 * owner + core}
+                    )
+
+            return
         z_in[q, chip] = value
 
         def body(step, carry):
@@ -414,10 +430,37 @@
 
         lax.fori_loop(1, ROWS // 2, body, 0)
 
+    def owns(q):
+        return (chip >= 3 * q) & (chip < 3 * q + 3)
+
+    def z_reduce(q):
+        @pl.when(owns(q))
+        def _():
+            wait_bytes(z_tile.at[q, pl.ds(0, ROWS // 2 - 1)], ar_recv.at[2, q])
+            slot = total.at[q, core, 3 * lat + chip - 3 * q]
+            slot[...] = jnp.sum(z_tile[q].astype(F32), axis=0).astype(BF16)
+
+            def body(step, carry):
+                chunk_start(slot, slot, 5, q, {"lon": lax.rem(me + 2 * step, ROWS)})
+                return carry
+
+            lax.fori_loop(1, ROWS // 2, body, 0)
+
     def z_finish(q):
-        wait_bytes(z_in.at[q, pl.ds(0, ROWS // 2 - 1)], ar_recv.at[2, q])
         mine = pl.ds(3 * lat, 3)
-        total[q, core, mine] = jnp.sum(z_in[q].astype(F32), axis=0).astype(BF16)
+        if q in SCATTERED:
+
+            @pl.when(owns(q))
+            def _():
+                wait_bytes(lat_sum.at[q, pl.ds(0, 2)], ar_recv.at[5, q])
+
+            @pl.when(jnp.logical_not(owns(q)))
+            def _():
+                wait_bytes(lat_sum.at[q], ar_recv.at[5, q])
+
+        else:
+            wait_bytes(z_in.at[q, pl.ds(0, ROWS // 2 - 1)], ar_recv.at[2, q])
+            total[q, core, mine] = jnp.sum(z_in[q].astype(F32), axis=0).astype(BF16)
         to_lat(lambda peer: total.at[q, core, mine], total.at[q, core, mine], 3, q)
 
     def gather_finish(q):
@@ -430,7 +473,19 @@
     def chunk_end(q):
         wait_bytes(total.at[q, 0], ar_send.at[0, q])
         wait_bytes(total.at[q, 0, pl.ds(0, 45)], ar_send.at[1, q])
-        wait_bytes(total.at[q, 0, pl.ds(0, 21)], ar_send.at[2, q])
+        if q in SCATTERED:
+
+            @pl.when(owns(q))
+            def _():
+                wait_bytes(total.at[q, 0, pl.ds(0, 2)], ar_send.at[2, q])
+                wait_bytes(total.at[q, 0, pl.ds(0, ROWS // 2 - 1)], ar_send.at[5, q])
+
+            @pl.when(jnp.logical_not(owns(q)))
+            def _():
+                wait_bytes(total.at[q, 0, pl.ds(0, 3)], ar_send.at[2, q])
+
+        else:
+            wait_bytes(total.at[q, 0, pl.ds(0, 21)], ar_send.at[2, q])
         wait_bytes(total.at[q, 0, pl.ds(0, 45)], ar_send.at[3, q])
         wait_bytes(total.at[q, 0], ar_send.at[4, q])
 
@@ -449,6 +504,8 @@
             parts[1 + h, c, 45:48] = jnp.zeros((3, 16, LANES), BF16)
     halo_middle(slab, tail, 0)
     STEP = 144
+    BATCH = 6
+    LAST = 7
     for copy in loads[1:]:
         copy.wait()
 
@@ -496,7 +553,7 @@
         lax.fori_loop(0, ROWS, activate, 0)
         if h == 1:
             halo_begin(pslab, ptail, 8)
-        spread_start(ps, g2, h, 2)
+        spread_start(ps, g2, h, 2, 0, ROWS - 1 if h == 0 else BATCH)
         own_piece(ps, g2, h)
 
     for k in range(3):
@@ -512,13 +569,18 @@
             )
     pair_start(0)
     halo_middle(pslab, ptail, 8)
+    pair_finish(0)
     fold(outs, folded, slice(0, CHANNELS))
     out_store = pltpu.make_async_copy(folded, out_ref, store_sem.at[0])
     out_store.start()
+    lat_finish(0)
+    spread_start(ps, g2, 1, 2, BATCH, ROWS - 1)
 
     for h in range(2):
         lanes = slice(h * LANES, (h + 1) * LANES)
         spread_wait(g2, h, 2)
+        if h == 1:
+            z_finish(0)
         to_spectrum(2, g2, h, cotspec)
 
         def back(n, carry):
@@ -537,28 +599,29 @@
 
         lax.fori_loop(0, WAVES // STEP, back, 0)
         pair_start(1 + h)
-        if h == 0:
-            pair_finish(0)
+        if h == 1:
+            pair_finish(2)
         to_field(3, zs, h)
         if h == 0:
-            spread_start(zs, s2, h, 3)
+            z_reduce(0)
+            spread_start(zs, s2, h, 3, 0, BATCH)
             own_piece(zs, s2, h)
             pair_finish(1)
             halo_wait_main(pslab, ptail, 8)
             inner_rows(vb, pslab, True)
-            lat_finish(0)
+            lat_finish(1)
+            spread_start(zs, s2, h, 3, BATCH, ROWS - 1)
         else:
-            pair_finish(2)
-            spread_start(zs, s2, h, 3, 0, 8)
+            spread_start(zs, s2, h, 3, 0, LAST)
             own_piece(zs, s2, h)
 
-    lat_finish(1)
     halo_wait_edge(pslab, ptail, 8)
     edge_rows(vb, pslab, True)
     lat_finish(2)
-    spread_start(zs, s2, 1, 3, 8, ROWS - 1)
+    spread_start(zs, s2, 1, 3, LAST, ROWS - 1)
+    z_finish(1)
+    gather_finish(0)
     mix(True)
-    z_finish(0)
 
     def finish(h):
         lanes = slice(h * LANES, (h + 1) * LANES)
@@ -577,28 +640,19 @@
         store.start()
         return store
 
-    z_finish(1)
-    finals = [finish(0)]
+    def chunk_out(q):
+        chunk_wait(q)
+        store = pltpu.make_async_copy(total.at[q], sum_ref.at[q], store_sem.at[3 + q])
+        store.start()
+        return store
+
     z_finish(2)
-    gather_finish(0)
+    finals = [chunk_out(0), finish(0)]
     gather_finish(1)
-    chunk_wait(0)
-    for k in range(3):
-        for c in range(2):
-            gw_ref[k, :, c * LANES : (c + 1) * LANES] = (
-                total[0, c, 16 * k : 16 * (k + 1)].reshape(CHANNELS, LANES).astype(F32)
-            )
-    def filter_out(h):
-        chunk_wait(1 + h)
-        for c in range(2):
-            gf_ref[c, :, h * LANES : (h + 1) * LANES] = (
-                total[1 + h, c, 0:45].reshape(WAVES, LANES).astype(F32)
-            )
-
-    filter_out(0)
+    finals.append(chunk_out(1))
     gather_finish(2)
     finals.append(finish(1))
-    filter_out(1)
+    finals.append(chunk_out(2))
 
     for phase, source in enumerate((xs, ys, ps, zs)):
         for h in range(2):
@@ -612,13 +666,36 @@
         store.wait()
 
 
-def deliver(*refs):
-    sources, targets, held, arrived, left = refs[0:4], refs[4:8], refs[8:12], refs[12], refs[13]
-    loads = [pltpu.make_async_copy(sources[i], held[i], arrived.at[i]) for i in range(4)]
-    stores = [pltpu.make_async_copy(held[i], targets[i], left.at[i]) for i in range(4)]
+def deliver(
+    out_ref, gin_ref, sum_ref, out_to, gin_to, gw_to, gf_to, out, gin, sums, gw, gf, arrived, left
+):
+    loads = [pltpu.make_async_copy(sum_ref.at[q], sums.at[q], arrived.at[q]) for q in range(3)]
+    loads.append(pltpu.make_async_copy(out_ref, out, arrived.at[3]))
+    loads.append(pltpu.make_async_copy(gin_ref, gin, arrived.at[4]))
+    stores = [
+        pltpu.make_async_copy(source, target, left.at[i])
+        for i, (source, target) in enumerate(
+            ((gw, gw_to), (gf.at[0], gf_to.at[0]), (gf.at[1], gf_to.at[1]), (out, out_to), (gin, gin_to))
+        )
+    ]
     for copy in loads:
         copy.start()
-    for i in range(4):
+    loads[0].wait()
+    for k in range(3):
+        for c in range(2):
+            gw[k, :, c * LANES : (c + 1) * LANES] = (
+                sums[0, c, 16 * k : 16 * (k + 1)].reshape(CHANNELS, LANES).astype(F32)
+            )
+    stores[0].start()
+    loads[1].wait()
+    loads[2].wait()
+    for c in range(2):
+        for h in range(2):
+            gf[c, :, h * LANES : (h + 1) * LANES] = (
+                sums[1 + h, c, 0:45].reshape(WAVES, LANES).astype(F32)
+            )
+        stores[1 + c].start()
+    for i in (3, 4):
         loads[i].wait()
         stores[i].start()
     for copy in stores:
@@ -630,16 +707,13 @@
     vmem = pl.BlockSpec(memory_space=pltpu.VMEM)
     hbm = pl.BlockSpec(memory_space=pl.ANY)
     pieces = (2, ROWS, PAD, LANES)
-    out, gin, gw, gf = pl.pallas_call(
+    field = jax.ShapeDtypeStruct((COLS, ROWS, CHANNELS), BF16)
+    sums = jax.ShapeDtypeStruct((3, 2, 48, 16, LANES), BF16)
+    results = pl.pallas_call(
         kernel,
-        out_shape=[
-            jax.ShapeDtypeStruct((COLS, ROWS, CHANNELS), BF16),
-            jax.ShapeDtypeStruct((COLS, ROWS, CHANNELS), BF16),
-            jax.ShapeDtypeStruct((3, CHANNELS, CHANNELS), F32),
-            jax.ShapeDtypeStruct((2, WAVES, CHANNELS), F32),
-        ],
+        out_shape=[field, field, sums],
         in_specs=[vmem, hbm, vmem, vmem] + [hbm] * 6,
-        out_specs=[hbm, hbm, vmem, vmem],
+        out_specs=[hbm, hbm, hbm],
         scratch_shapes=[
             pltpu.VMEM((4, ROWS * PAD, ROWS * PAD), BF16),
             pltpu.VMEM((COLS, ROWS, CHANNELS), BF16),
@@ -671,15 +745,16 @@
             pltpu.VMEM((3, ROWS, 3, 16, LANES), BF16),
             pltpu.VMEM((3, 3, 16, LANES), BF16),
             pltpu.VMEM((3, ROWS // 2, 3, 16, LANES), BF16),
+            pltpu.VMEM((3, ROWS // 2, 16, LANES), BF16),
             pltpu.VMEM((3, 2, 48, 16, LANES), BF16),
             pltpu.SemaphoreType.DMA((7,)),
-            pltpu.SemaphoreType.DMA((3,)),
+            pltpu.SemaphoreType.DMA((6,)),
             pltpu.SemaphoreType.DMA((4, 2)),
             pltpu.SemaphoreType.DMA((4, 2)),
             pltpu.SemaphoreType.DMA((16,)),
             pltpu.SemaphoreType.DMA((16,)),
-            pltpu.SemaphoreType.DMA((5, 3)),
-            pltpu.SemaphoreType.DMA((5, 3)),
+            pltpu.SemaphoreType.DMA((6, 3)),
+            pltpu.SemaphoreType.DMA((6, 3)),
         ],
         compiler_params=pltpu.CompilerParams(
             collective_id=0, has_side_effects=True, vmem_limit_bytes=60 * 1024 * 1024
@@ -696,14 +771,21 @@
         spectral_filter,
         *tables,
     )
-    results = (out, gin, gw, gf)
+    shapes = [
+        field,
+        field,
+        jax.ShapeDtypeStruct((3, CHANNELS, CHANNELS), F32),
+        jax.ShapeDtypeStruct((2, WAVES, CHANNELS), F32),
+    ]
+    held = [field, field, sums] + shapes[2:]
     out, gin, gw, gf = pl.pallas_call(
         deliver,
-        out_shape=[jax.ShapeDtypeStruct(r.shape, r.dtype) for r in results],
-        in_specs=[hbm] * 4,
+        out_shape=shapes,
+        in_specs=[hbm] * 3,
         out_specs=[hbm] * 4,
-        scratch_shapes=[pltpu.VMEM(r.shape, r.dtype) for r in results]
-        + [pltpu.SemaphoreType.DMA((4,)), pltpu.SemaphoreType.DMA((4,))],
+        scratch_shapes=[pltpu.VMEM(r.shape, r.dtype) for r in held]
+        + [pltpu.SemaphoreType.DMA((5,)), pltpu.SemaphoreType.DMA((5,))],
+        compiler_params=pltpu.CompilerParams(vmem_limit_bytes=60 * 1024 * 1024),
     )(*results)
     return (jnp.transpose(out, (1, 0, 2)), jnp.transpose(gin, (1, 0, 2)), gw, gf)
 

time: 106 us -> 103 us (0.972)
  Pallas kernels: 106 us -> 103 us
    pallas_call x2, Pallas kernels: 106 us -> 103 us  [the longest x1 99.5 us: on_device(): pl.pallas_call(kernel, out_shape=[field, field, sums], in_specs=[vmem, hb...]
where the time goes in v4:
time: 103 us
  Pallas kernels  103 us (100%)
    pallas_call x1, Pallas kernels, on_device(): pl.pallas_call(kernel, out_shape=[field, field, sums], in_specs=[vmem, hb...  99.5 us
    pallas_call x1, Pallas kernels, on_device(): pl.pallas_call(deliver, out_shape=shapes, in_specs=[hbm] * 3, out_specs=[...  2.99 us

profile of v4, /device:TPU:1, one launch (start us, length us, event | category | flops | bytes accessed | tf_op | source)
XLA Modules:
  0.0 103.2 jit_solution(11231957697163843862)
XLA Ops:
  0.6 99.5 %shard_map.129 = (bf16[90,16,256]{2,1,0:T(8,128)(2,1)}, bf16[90,16,256]{2,1,0:T(8,128)(2,1)}, bf16[3,2,48,16,128]{4,3,2,1,0:T(8,128)(2,1)}) custom-call(bf16[90,16,256]{2,1,0:T(8,128)(2,1)} %bitcast.6, bf16[90,16,256]{2,1,0:T(8,128)(2,1)} %bitcast.7, bf16[3,3,33,256]{3,2,1,0:T(8,128)(2,1)} %bitcast.10, s32[1,256]{1,0:T(1,128)} %bitcast.11, ...), custom_call_target="tpu_custom_call" | custom-call | flops 8000000000 | bytes 30000000 | tf_op jit(solution)/shard_map/pallas_call | solution.py:712
  100.2 3.0 %shard_map.130 = (bf16[90,16,256]{2,1,0:T(8,128)(2,1)}, bf16[90,16,256]{2,1,0:T(8,128)(2,1)}, f32[3,256,256]{2,1,0:T(8,128)}, f32[2,720,256]{2,1,0:T(8,128)}) custom-call(bf16[90,16,256]{2,1,0:T(8,128)(2,1)} %get-tuple-element.11.out_ref, bf16[90,16,256]{2,1,0:T(8,128)(2,1)} %get-tuple-element.12.gin_ref, bf16[3,2,48,16,128]{4,3,2,1,0:T(8,128)(2,1)} %get-tuple-element.13.sum_ref), custom_call_target="tpu_custom_call" | custom-call | tf_op jit(solution)/shard_map/pallas_call | solution.py:781

commit v5 on v4

--- a/solution.py
+++ b/solution.py
@@ -678,8 +678,11 @@
             ((gw, gw_to), (gf.at[0], gf_to.at[0]), (gf.at[1], gf_to.at[1]), (out, out_to), (gin, gin_to))
         )
     ]
-    for copy in loads:
-        copy.start()
+    for i in (3, 4, 0, 1, 2):
+        loads[i].start()
+    for i in (3, 4):
+        loads[i].wait()
+        stores[i].start()
     loads[0].wait()
     for k in range(3):
         for c in range(2):
@@ -695,9 +698,6 @@
                 sums[1 + h, c, 0:45].reshape(WAVES, LANES).astype(F32)
             )
         stores[1 + c].start()
-    for i in (3, 4):
-        loads[i].wait()
-        stores[i].start()
     for copy in stores:
         copy.wait()
 

time: 103 us -> 103 us (level)
  no operation moved by 1% of the time
where the time goes in v5:
time: 103 us
  Pallas kernels  103 us (100%)
    pallas_call x1, Pallas kernels, on_device(): pl.pallas_call(kernel, out_shape=[field, field, sums], in_specs=[vmem, hb...  99.5 us
    pallas_call x1, Pallas kernels, on_device(): pl.pallas_call(deliver, out_shape=shapes, in_specs=[hbm] * 3, out_specs=[...  3.06 us

profile of v5, /device:TPU:1, one launch (start us, length us, event | category | flops | bytes accessed | tf_op | source)
XLA Modules:
  0.0 103.2 jit_solution(726742293838256619)
XLA Ops:
  0.6 99.5 %shard_map.129 = (bf16[90,16,256]{2,1,0:T(8,128)(2,1)}, bf16[90,16,256]{2,1,0:T(8,128)(2,1)}, bf16[3,2,48,16,128]{4,3,2,1,0:T(8,128)(2,1)}) custom-call(bf16[90,16,256]{2,1,0:T(8,128)(2,1)} %bitcast.6, bf16[90,16,256]{2,1,0:T(8,128)(2,1)} %bitcast.7, bf16[3,3,33,256]{3,2,1,0:T(8,128)(2,1)} %bitcast.10, s32[1,256]{1,0:T(1,128)} %bitcast.11, ...), custom_call_target="tpu_custom_call" | custom-call | flops 8000000000 | bytes 30000000 | tf_op jit(solution)/shard_map/pallas_call | solution.py:712
  100.2 3.1 %shard_map.130 = (bf16[90,16,256]{2,1,0:T(8,128)(2,1)}, bf16[90,16,256]{2,1,0:T(8,128)(2,1)}, f32[3,256,256]{2,1,0:T(8,128)}, f32[2,720,256]{2,1,0:T(8,128)}) custom-call(bf16[90,16,256]{2,1,0:T(8,128)(2,1)} %get-tuple-element.11.out_ref, bf16[90,16,256]{2,1,0:T(8,128)(2,1)} %get-tuple-element.12.gin_ref, bf16[3,2,48,16,128]{4,3,2,1,0:T(8,128)(2,1)} %get-tuple-element.13.sum_ref), custom_call_target="tpu_custom_call" | custom-call | tf_op jit(solution)/shard_map/pallas_call | solution.py:781
